TPU v7x, 128 devices: a whole 4x4x4 slice. The times are simulated.
128 devices in a mesh: dp: 64 (over x, y, z_lo, core), expert: 2 (over z_hi).
Axes of the slice: x: 4, y: 4, z: 4 (z_hi: 2, z_lo: 2; z = z_hi * 2 + z_lo), core: 2. Of those that a mesh axis runs over, the one named last changes fastest.
Arguments:
- inputs: bfloat16 [49152, 1536], P(('dp', 'expert')), may hold values from -6 to 6
- cotangent: bfloat16 [49152, 1536], P(('dp', 'expert')), may hold values from -24 to 24
- norm_one: float32 [1536], replicated, may hold values from 0.5 to 1.5
- kv_weight: bfloat16 [1536, 1024], replicated, may hold values from -0.15625 to 0.15625
- attn_router: bfloat16 [1536, 8], replicated, may hold values from -0.109375 to 0.109375
- query_experts: bfloat16 [8, 1536, 512], P('expert'), may hold values from -0.15625 to 0.15625
- out_experts: bfloat16 [8, 512, 1536], P('expert'), may hold values from -2 to 2
- norm_two: float32 [1536], replicated, may hold values from 0.5 to 1.5
- mlp_router: bfloat16 [1536, 8], replicated, may hold values from -0.109375 to 0.109375
- gate_experts: bfloat16 [8, 1536, 512], P('expert'), may hold values from -0.15625 to 0.15625
- up_experts: bfloat16 [8, 1536, 512], P('expert'), may hold values from -0.15625 to 0.15625
- down_experts: bfloat16 [8, 512, 1536], P('expert'), may hold values from -0.25 to 0.25
- attn_routes: int32 [64, 2, 384, 2], P('dp'), may hold values from 0 to 7, all different within a row
- mlp_routes: int32 [64, 2, 384, 2], P('dp'), may hold values from 0 to 7, all different within a row
- slot_order: int32 [64, 2, 2, 768], P('dp'), may hold values from 0 to 767, each once within a row
- seg_lengths: int32 [64, 2, 13], P('dp'), may hold values from 12 to 240, as said below
- seg_parents: int32 [64, 2, 13], P('dp'), may hold values from 0 to 4, as said below
Outputs:
- output: bfloat16 [49152, 1536], P(('dp', 'expert'))
- input_grad: bfloat16 [49152, 1536], P(('dp', 'expert'))
- norm_one_grad: float32 [1536], P(('dp', 'expert'))
- kv_weight_grad: float32 [1536, 1024], P(('dp', 'expert'))
- attn_router_grad: float32 [1536, 8], P(('dp', 'expert'))
- query_grad: float32 [8, 1536, 512], P('expert', 'dp')
- out_grad: float32 [8, 512, 1536], P('expert', 'dp')
- norm_two_grad: float32 [1536], P(('dp', 'expert'))
- mlp_router_grad: float32 [1536, 8], P(('dp', 'expert'))
- gate_grad: float32 [8, 1536, 512], P('expert', 'dp')
- up_grad: float32 [8, 1536, 512], P('expert', 'dp')
- down_grad: float32 [8, 512, 1536], P('expert', 'dp')
Inputs may be any that keep to these rules, and one draw needn't show every extreme that they name: `attn_routes`: each token names 2 different experts. `mlp_routes`: each token names 2 different experts. `slot_order`: for each tree and sub-layer, every pair index appears once. `seg_lengths`: a tree's 13 lengths sum to 384; segment 0, the trunk, is the longest. `seg_parents`: segment 0 is its own parent; segments 1 to 4 have parent 0; each of them is the parent of exactly two of segments 5 to 12.
All inputs are finite; a program needn't handle non-finite values.
Results may differ from a plain program's by a relative error of at most 0.015.
Values may be sent and summed in bfloat16 or wider, within the bound.
A program may use at most 256 MiB of HBM per device.

v0:
```python
from functools import partial

import jax
import jax.numpy as jnp
from jax import lax
from jax.sharding import PartitionSpec as P

D = 1536
HD = 64
KVH = 8
FF = 512
QW = 512
EA = 8
EM = 8
TOPK = 2
NSEG = 13
TOK_DEV = 384
CAP = 120


epsilon = 1e-06


def rotary(values, position, direction):
    row_total = values.shape[0]
    halves = values.reshape(row_total, KVH, 2, HD // 2)
    frequency = 10000.0 ** (-2.0 * jnp.arange(HD // 2).astype(jnp.float32) / HD)
    angles = position.astype(jnp.float32)[:, None] * frequency[None, :]
    cosine = jnp.cos(angles)[:, None, :]
    sine_term = direction * jnp.sin(angles)[:, None, :]
    first_half = halves[:, :, 0] * cosine - halves[:, :, 1] * sine_term
    second_half = halves[:, :, 1] * cosine + halves[:, :, 0] * sine_term
    return jnp.stack([first_half, second_half], axis=2).reshape(row_total, KVH * HD)


def tree_tables(lengths, parents):
    token_ids = jnp.arange(TOK_DEV, dtype=jnp.int32)
    starts = jnp.cumsum(lengths) - lengths
    segment = jnp.sum((token_ids[:, None] >= starts[None, :]).astype(jnp.int32), axis=1) - 1
    seg_ids = jnp.arange(NSEG, dtype=jnp.int32)
    grand_parents = jnp.sum(
        jnp.where(parents[:, None] == seg_ids[None, :], parents[None, :], 0), axis=1
    )
    ancestor = (
        (seg_ids[:, None] == seg_ids[None, :])
        | (parents[:, None] == seg_ids[None, :])
        | (grand_parents[:, None] == seg_ids[None, :])
    )
    member = (segment[:, None] == seg_ids[None, :]).astype(jnp.int32)
    reachable = jnp.dot(jnp.dot(member, ancestor.astype(jnp.int32)), member.T)
    allowed = (reachable > 0) & (token_ids[None, :] <= token_ids[:, None])
    position = jnp.sum(allowed.astype(jnp.int32), axis=1) - 1
    return (allowed, position)


def slot_table(routes, priority, expert_count):
    pair_expert = routes.reshape(-1)
    ordered = jnp.take(pair_expert, priority)
    onehot = (ordered[:, None] == jnp.arange(expert_count, dtype=jnp.int32)[None, :]).astype(
        jnp.int32
    )
    earlier = jnp.cumsum(onehot, axis=0) - onehot
    ranked = jnp.sum(earlier * onehot, axis=1)
    slot_index = jnp.zeros_like(ranked).at[priority].set(ranked)
    flat_slot = jnp.where(slot_index < CAP, pair_expert * CAP + slot_index, expert_count * CAP)
    owner_pair = (
        jnp.full((expert_count * CAP,), TOPK * TOK_DEV, jnp.int32)
        .at[flat_slot]
        .set(jnp.arange(TOPK * TOK_DEV, dtype=jnp.int32), mode="drop")
    )
    return (flat_slot, owner_pair)


def pick_gates(logits, routes, expert_count):
    choose = (
        routes[:, :, None] == jnp.arange(expert_count, dtype=jnp.int32)[None, None, :]
    ).astype(jnp.float32)
    picked = jnp.sum(choose * logits[:, None, :], axis=-1)
    return (jax.nn.softmax(picked, axis=-1), choose)


def gather_rows(source_rows, row_index):
    padded = jnp.concatenate(
        [source_rows, jnp.zeros((1,) + source_rows.shape[1:], source_rows.dtype)]
    )
    return jnp.take(padded, row_index, axis=0)


def router_back(gates, grad_gates, choose):
    picked_grad = gates * (grad_gates - jnp.sum(gates * grad_gates, axis=-1, keepdims=True))
    return jnp.sum(choose * picked_grad[:, :, None], axis=1).astype(jnp.bfloat16)


def per_device(
    inputs,
    cotangent,
    norm_one,
    kv_weight,
    attn_router,
    query_experts,
    out_experts,
    norm_two,
    mlp_router,
    gate_experts,
    up_experts,
    down_experts,
    attn_routes,
    mlp_routes,
    slot_order,
    seg_lengths,
    seg_parents,
):
    members = lax.axis_size("expert")
    my_index = lax.axis_index("expert")
    local_attn = query_experts.shape[0]
    local_mlp = gate_experts.shape[0]
    row_count = local_attn * CAP
    score_scale = HD ** (-0.5)

    def select_own(stacked):
        return lax.dynamic_index_in_dim(stacked, my_index, 0, keepdims=False)

    allowed, position = jax.vmap(tree_tables)(seg_lengths[0], seg_parents[0])
    flat_attn, owner_attn = jax.vmap(partial(slot_table, expert_count=EA))(
        attn_routes[0], slot_order[0, :, 0]
    )
    own_flat_attn = select_own(flat_attn)
    own_owner_attn = select_own(owner_attn)
    own_position = select_own(position)
    own_flat_mlp, own_owner_mlp = slot_table(
        select_own(mlp_routes[0]), select_own(slot_order[0, :, 1]), EM
    )
    input_float = inputs.astype(jnp.float32)
    inverse_one = lax.rsqrt(jnp.mean(input_float * input_float, axis=-1, keepdims=True) + epsilon)
    normed = (input_float * inverse_one * norm_one).astype(jnp.bfloat16)
    key_value = jnp.dot(normed, kv_weight, preferred_element_type=jnp.float32)
    key_rows = rotary(key_value[:, :QW], own_position, 1.0).astype(jnp.bfloat16)
    value_rows = key_value[:, QW:].astype(jnp.bfloat16)
    attn_gates, attn_choose = pick_gates(
        jnp.dot(normed, attn_router, preferred_element_type=jnp.float32),
        select_own(attn_routes[0]),
        EA,
    )
    attn_send = gather_rows(normed, own_owner_attn // TOPK).reshape(EA, CAP, D)
    attn_recv = lax.all_to_all(
        attn_send, "expert", split_axis=0, concat_axis=0, tiled=True
    ).reshape(members, local_attn, CAP, D)
    both_keys, both_values = (
        lax.all_gather(key_rows, "expert", axis=0, tiled=True),
        lax.all_gather(value_rows, "expert", axis=0, tiled=True),
    )
    key_tree = both_keys.reshape(members, TOK_DEV, KVH, HD)
    value_tree = both_values.reshape(members, TOK_DEV, KVH, HD)
    token_table = (owner_attn // TOPK).reshape(members, EA, CAP)
    my_tokens = lax.dynamic_slice_in_dim(token_table, my_index * local_attn, local_attn, 1).reshape(
        members, row_count
    )
    my_tokens = jnp.where(my_tokens < TOK_DEV, my_tokens, 0)
    row_position = jax.vmap(jnp.take)(position, my_tokens)
    row_mask = jax.vmap(partial(jnp.take, axis=0))(allowed, my_tokens)
    query_pre = jnp.einsum(
        "slcd,ldq->slcq", attn_recv, query_experts, preferred_element_type=jnp.float32
    )
    queries = (
        rotary(query_pre.reshape(members * row_count, QW), row_position.reshape(-1), 1.0)
        .astype(jnp.bfloat16)
        .reshape(members, row_count, KVH, HD)
    )

    def score_block():
        raw_scores = (
            jnp.einsum("srhd,sthd->shrt", queries, key_tree, preferred_element_type=jnp.float32)
            * score_scale
        )
        return jnp.where(row_mask[:, None], raw_scores, -1e30)

    scores = score_block()
    top_score = jnp.max(scores, axis=-1, keepdims=True)
    exponent = jnp.exp(scores - top_score)
    totals = jnp.sum(exponent, axis=-1, keepdims=True)
    log_total = top_score + jnp.log(totals)
    attended = jnp.einsum(
        "shrt,sthd->srhd",
        (exponent / totals).astype(jnp.bfloat16),
        value_tree,
        preferred_element_type=jnp.float32,
    )
    attended = attended.astype(jnp.bfloat16).reshape(members, local_attn, CAP, QW)
    out_rows = jnp.einsum(
        "slcq,lqd->slcd", attended, out_experts, preferred_element_type=jnp.float32
    ).astype(jnp.bfloat16)
    attn_back = lax.all_to_all(
        out_rows.reshape(members * local_attn, CAP, D),
        "expert",
        split_axis=0,
        concat_axis=0,
        tiled=True,
    )
    attn_pairs = (
        gather_rows(attn_back.reshape(EA * CAP, D), own_flat_attn)
        .reshape(TOK_DEV, TOPK, D)
        .astype(jnp.float32)
    )
    middle = input_float + jnp.sum(attn_gates[:, :, None] * attn_pairs, axis=1)
    inverse_two = lax.rsqrt(jnp.mean(middle * middle, axis=-1, keepdims=True) + epsilon)
    normed_two = (middle * inverse_two * norm_two).astype(jnp.bfloat16)
    mlp_gates, mlp_choose = pick_gates(
        jnp.dot(normed_two, mlp_router, preferred_element_type=jnp.float32),
        select_own(mlp_routes[0]),
        EM,
    )
    mlp_send = gather_rows(normed_two, own_owner_mlp // TOPK).reshape(EM, CAP, D)
    slot_rows = lax.all_to_all(mlp_send, "expert", split_axis=0, concat_axis=0, tiled=True)
    count_items = slot_rows.shape[1]
    grouped = slot_rows.reshape(members, local_mlp, count_items, D)
    gate_part = jnp.einsum(
        "slnd,ldf->slnf", grouped, gate_experts, preferred_element_type=jnp.float32
    )
    up_part = jnp.einsum("slnd,ldf->slnf", grouped, up_experts, preferred_element_type=jnp.float32)
    hidden_part = (jax.nn.silu(gate_part) * up_part).astype(jnp.bfloat16)
    result = jnp.einsum(
        "slnf,lfd->slnd", hidden_part, down_experts, preferred_element_type=jnp.float32
    ).astype(jnp.bfloat16)
    returned = lax.all_to_all(
        result.reshape(members * local_mlp, count_items, D),
        "expert",
        split_axis=0,
        concat_axis=0,
        tiled=True,
    )
    flat_shape = (members * local_mlp, count_items, FF)
    gate_pre = gate_part.reshape(flat_shape)
    up_pre = up_part.reshape(flat_shape)
    hidden = hidden_part.reshape(flat_shape)
    mlp_pairs = (
        gather_rows(returned.reshape(EM * CAP, D), own_flat_mlp)
        .reshape(TOK_DEV, TOPK, D)
        .astype(jnp.float32)
    )
    output = (middle + jnp.sum(mlp_gates[:, :, None] * mlp_pairs, axis=1)).astype(jnp.bfloat16)
    grad_final = cotangent.astype(jnp.float32)
    grad_mlp_gates = jnp.sum(grad_final[:, None, :] * mlp_pairs, axis=-1)
    mlp_grad_rows = (
        (mlp_gates[:, :, None] * grad_final[:, None, :])
        .astype(jnp.bfloat16)
        .reshape(TOPK * TOK_DEV, D)
    )
    mlp_grad_send = gather_rows(mlp_grad_rows, own_owner_mlp).reshape(EM, CAP, D)
    mlp_grad_recv = lax.all_to_all(
        mlp_grad_send, "expert", split_axis=0, concat_axis=0, tiled=True
    ).reshape(members, local_mlp, CAP, D)
    grouped_shape = (members, local_mlp, CAP, FF)
    gate_grouped = gate_pre.reshape(grouped_shape)
    up_grouped = up_pre.reshape(grouped_shape)
    grad_hidden = jnp.einsum(
        "slcd,lfd->slcf", mlp_grad_recv, down_experts, preferred_element_type=jnp.float32
    )
    grad_down = jnp.einsum(
        "slcf,slcd->lfd",
        hidden.reshape(grouped_shape),
        mlp_grad_recv,
        preferred_element_type=jnp.float32,
    )
    sigmoid_gate = jax.nn.sigmoid(gate_grouped)
    grad_gate_pre = (
        grad_hidden * up_grouped * sigmoid_gate * (1.0 + gate_grouped * (1.0 - sigmoid_gate))
    ).astype(jnp.bfloat16)
    grad_up_pre = (grad_hidden * gate_grouped * sigmoid_gate).astype(jnp.bfloat16)
    mlp_rows_grouped = slot_rows.reshape(members, local_mlp, CAP, D)
    grad_gate = jnp.einsum(
        "slcd,slcf->ldf", mlp_rows_grouped, grad_gate_pre, preferred_element_type=jnp.float32
    )
    grad_up = jnp.einsum(
        "slcd,slcf->ldf", mlp_rows_grouped, grad_up_pre, preferred_element_type=jnp.float32
    )
    grad_mlp_rows = jnp.einsum(
        "slcf,ldf->slcd", grad_gate_pre, gate_experts, preferred_element_type=jnp.float32
    )
    grad_mlp_rows = (
        grad_mlp_rows
        + jnp.einsum("slcf,ldf->slcd", grad_up_pre, up_experts, preferred_element_type=jnp.float32)
    ).astype(jnp.bfloat16)
    grad_mlp_back = lax.all_to_all(
        grad_mlp_rows.reshape(members * local_mlp, CAP, D),
        "expert",
        split_axis=0,
        concat_axis=0,
        tiled=True,
    )
    grad_normed_two = jnp.sum(
        gather_rows(grad_mlp_back.reshape(EM * CAP, D), own_flat_mlp)
        .reshape(TOK_DEV, TOPK, D)
        .astype(jnp.float32),
        axis=1,
    )
    grad_mlp_logits = router_back(mlp_gates, grad_mlp_gates, mlp_choose)
    grad_mlp_router = jnp.einsum(
        "td,te->de", normed_two, grad_mlp_logits, preferred_element_type=jnp.float32
    )
    grad_normed_two = grad_normed_two + jnp.einsum(
        "te,de->td", grad_mlp_logits, mlp_router, preferred_element_type=jnp.float32
    )
    weighted_two = grad_normed_two * norm_two
    grad_middle = (
        grad_final
        + inverse_two * weighted_two
        - middle
        * (inverse_two * inverse_two * inverse_two)
        * jnp.mean(weighted_two * middle, axis=-1, keepdims=True)
    )
    grad_norm_two = jnp.sum(grad_normed_two * middle * inverse_two, axis=0)
    grad_attn_gates = jnp.sum(grad_middle[:, None, :] * attn_pairs, axis=-1)
    attn_grad_rows = (
        (attn_gates[:, :, None] * grad_middle[:, None, :])
        .astype(jnp.bfloat16)
        .reshape(TOPK * TOK_DEV, D)
    )
    attn_grad_send = gather_rows(attn_grad_rows, own_owner_attn).reshape(EA, CAP, D)
    attn_grad_recv = lax.all_to_all(
        attn_grad_send, "expert", split_axis=0, concat_axis=0, tiled=True
    ).reshape(members, local_attn, CAP, D)
    grad_attended = jnp.einsum(
        "slcd,lqd->slcq", attn_grad_recv, out_experts, preferred_element_type=jnp.float32
    ).astype(jnp.bfloat16)
    grad_out = jnp.einsum(
        "slcq,slcd->lqd", attended, attn_grad_recv, preferred_element_type=jnp.float32
    )
    prob_float = jnp.exp(score_block() - log_total)
    grad_heads = grad_attended.reshape(members, row_count, KVH, HD)
    grad_values_part = jnp.einsum(
        "shrt,srhd->sthd",
        prob_float.astype(jnp.bfloat16),
        grad_heads,
        preferred_element_type=jnp.float32,
    )
    grad_probs = jnp.einsum(
        "srhd,sthd->shrt", grad_heads, value_tree, preferred_element_type=jnp.float32
    )
    grad_scores = (
        prob_float * (grad_probs - jnp.sum(grad_probs * prob_float, axis=-1, keepdims=True))
    ).astype(jnp.bfloat16)
    grad_queries = score_scale * jnp.einsum(
        "shrt,sthd->srhd", grad_scores, key_tree, preferred_element_type=jnp.float32
    )
    grad_keys_part = score_scale * jnp.einsum(
        "shrt,srhd->sthd", grad_scores, queries, preferred_element_type=jnp.float32
    )
    grad_query_pre = (
        rotary(grad_queries.reshape(members * row_count, QW), row_position.reshape(-1), -1.0)
        .astype(jnp.bfloat16)
        .reshape(members, local_attn, CAP, QW)
    )
    grad_query = jnp.einsum(
        "slcd,slcq->ldq", attn_recv, grad_query_pre, preferred_element_type=jnp.float32
    )
    grad_attn_rows = jnp.einsum(
        "slcq,ldq->slcd", grad_query_pre, query_experts, preferred_element_type=jnp.float32
    ).astype(jnp.bfloat16)
    grad_attn_back = lax.all_to_all(
        grad_attn_rows.reshape(members * local_attn, CAP, D),
        "expert",
        split_axis=0,
        concat_axis=0,
        tiled=True,
    )
    grad_keys_tree, grad_values_tree = (
        lax.psum_scatter(
            grad_keys_part.reshape(members * TOK_DEV, QW).astype(jnp.bfloat16),
            "expert",
            scatter_dimension=0,
            tiled=True,
        ).astype(jnp.float32),
        lax.psum_scatter(
            grad_values_part.reshape(members * TOK_DEV, QW).astype(jnp.bfloat16),
            "expert",
            scatter_dimension=0,
            tiled=True,
        ).astype(jnp.float32),
    )
    grad_key_value = jnp.concatenate(
        [rotary(grad_keys_tree, own_position, -1.0), grad_values_tree], axis=1
    ).astype(jnp.bfloat16)
    grad_kv = jnp.einsum("td,tk->dk", normed, grad_key_value, preferred_element_type=jnp.float32)
    grad_attn_logits = router_back(attn_gates, grad_attn_gates, attn_choose)
    grad_attn_router = jnp.einsum(
        "td,te->de", normed, grad_attn_logits, preferred_element_type=jnp.float32
    )
    grad_normed = jnp.einsum(
        "tk,dk->td", grad_key_value, kv_weight, preferred_element_type=jnp.float32
    )
    grad_normed = grad_normed + jnp.sum(
        gather_rows(grad_attn_back.reshape(EA * CAP, D), own_flat_attn)
        .reshape(TOK_DEV, TOPK, D)
        .astype(jnp.float32),
        axis=1,
    )
    grad_normed = grad_normed + jnp.einsum(
        "te,de->td", grad_attn_logits, attn_router, preferred_element_type=jnp.float32
    )
    weighted_one = grad_normed * norm_one
    grad_input = (
        grad_middle
        + inverse_one * weighted_one
        - input_float
        * (inverse_one * inverse_one * inverse_one)
        * jnp.mean(weighted_one * input_float, axis=-1, keepdims=True)
    )
    grad_norm_one = jnp.sum(grad_normed * input_float * inverse_one, axis=0)
    shared = (
        lax.psum_scatter(grad_norm_one, ("dp", "expert"), scatter_dimension=0, tiled=True),
        lax.psum_scatter(grad_kv, ("dp", "expert"), scatter_dimension=0, tiled=True),
        lax.psum_scatter(grad_attn_router, ("dp", "expert"), scatter_dimension=0, tiled=True),
        lax.psum_scatter(grad_norm_two, ("dp", "expert"), scatter_dimension=0, tiled=True),
        lax.psum_scatter(grad_mlp_router, ("dp", "expert"), scatter_dimension=0, tiled=True),
    )
    expert_grads = (
        lax.psum_scatter(grad_query, "dp", scatter_dimension=1, tiled=True),
        lax.psum_scatter(grad_out, "dp", scatter_dimension=1, tiled=True),
        lax.psum_scatter(grad_gate, "dp", scatter_dimension=1, tiled=True),
        lax.psum_scatter(grad_up, "dp", scatter_dimension=1, tiled=True),
        lax.psum_scatter(grad_down, "dp", scatter_dimension=1, tiled=True),
    )
    return (
        output,
        grad_input.astype(jnp.bfloat16),
        shared[0],
        shared[1],
        shared[2],
        expert_grads[0],
        expert_grads[1],
        shared[3],
        shared[4],
        expert_grads[2],
        expert_grads[3],
        expert_grads[4],
    )


def solution(mesh):
    placed = (
        P(("dp", "expert"), None),
        P(("dp", "expert"), None),
        P(),
        P(),
        P(),
        P("expert", None, None),
        P("expert", None, None),
        P(),
        P(),
        P("expert", None, None),
        P("expert", None, None),
        P("expert", None, None),
        P("dp", None, None, None),
        P("dp", None, None, None),
        P("dp", None, None, None),
        P("dp", None, None),
        P("dp", None, None),
    )
    return jax.shard_map(
        per_device,
        mesh=mesh,
        in_specs=placed,
        out_specs=(
            P(("dp", "expert"), None),
            P(("dp", "expert"), None),
            P(("dp", "expert")),
            P(("dp", "expert"), None),
            P(("dp", "expert"), None),
            P("expert", "dp", None),
            P("expert", "dp", None),
            P(("dp", "expert")),
            P(("dp", "expert"), None),
            P("expert", "dp", None),
            P("expert", "dp", None),
            P("expert", "dp", None),
        ),
        check_vma=False,
    )
```

profile of v0, /device:TPU:1, one launch (start us, length us, event | category | flops | bytes accessed | tf_op | source)
XLA Modules:
  0.0 2317.4 jit_solution(18066067554508372114)
XLA Ops:
  12.0 13.4 gather_fusion.1
  85.7 10.5 gather_fusion.3
  96.3 12.2 gather_fusion.2
  113.7 13.5 all_gather.7
  129.9 11.8 all_gather.6
  214.1 24.4 %all-to-all-done.1 = bf16[8,120,1536]{2,1,0:T(8,128)(2,1)} async-done(((bf16[8,120,1536]{2,1,0:T(8,128)(2,1)}), bf16[8,120,1536]{2,1,0:T(8,128)(2,1)}, u32[]{:S(2)}, u32[]{:S(2)}) %all-to-all-start.1) | async-done | bytes 2949152 | tf_op jit(solution)/shard_map/all_to_all | solution.py:192
  261.3 11.0 multiply_reduce_fusion.4
  289.7 35.2 %all_to_all.40 = bf16[8,120,1536]{2,1,0:T(8,128)(2,1)S(1)} all-to-all(bf16[8,120,1536]{2,1,0:T(8,128)(2,1)S(1)} %bitcast.280), channel_id=1, replica_groups=mesh['dp'=64,'expert'=2] {'expert'}, dimensions={0} | all-to-all | bytes 5898240 | tf_op jit(solution)/shard_map/all_to_all | solution.py:213
  357.3 17.0 all-to-all-done.3
  399.1 9.2 gather_fusion.8
  410.6 33.5 %all_to_all.41 = bf16[8,120,1536]{2,1,0:T(8,128)(2,1)S(1)} all-to-all(bf16[8,120,1536]{2,1,0:T(8,128)(2,1)S(1)} %bitcast.281), channel_id=1, replica_groups=mesh['dp'=64,'expert'=2] {'expert'}, dimensions={0} | all-to-all | bytes 5898240 | tf_op jit(solution)/shard_map/all_to_all | solution.py:249
  466.3 27.6 %all-to-all-done.5 = bf16[8,120,1536]{2,1,0:T(8,128)(2,1)} async-done(((bf16[8,120,1536]{2,1,0:T(8,128)(2,1)}), bf16[8,120,1536]{2,1,0:T(8,128)(2,1)}, u32[]{:S(2)}, u32[]{:S(2)}) %all-to-all-start.5) | async-done | bytes 2949152 | tf_op jit(solution)/shard_map/all_to_all | solution.py:283
  518.8 9.4 reduce_sum.261
  540.4 11.0 multiply_reduce_fusion.3
  574.8 9.2 gather_fusion.10
  593.1 28.7 %all-to-all-done.6 = bf16[8,120,1536]{2,1,0:T(8,128)(2,1)} async-done(((bf16[8,120,1536]{2,1,0:T(8,128)(2,1)}), bf16[8,120,1536]{2,1,0:T(8,128)(2,1)}, u32[]{:S(2)}, u32[]{:S(2)}) %all-to-all-start.6) | async-done | bytes 2949152 | tf_op jit(solution)/shard_map/all_to_all | solution.py:319
  702.6 16.7 all-to-all-done.7
  742.3 9.4 reduce_sum.268
  811.5 423.7 %fusion = f32[16,1024]{1,0:T(8,128)S(1)} fusion(f32[1536,1024]{1,0:T(8,128)} %fusion.115), kind=kCustom, calls=%all-reduce-scatter | all-reduce-scatter fusion | flops 2097153 | bytes 6356992
  1257.7 10.2 collective-permute-start.22
  1342.4 49.5 %concatenate.48 = f32[524,1024]{1,0:T(8,128)} concatenate(f32[12,1024]{1,0:T(8,128)S(1)} %collective-permute-done.31, f32[16,1024]{1,0:T(8,128)S(1)} %collective-permute-done.30, f32[16,1024]{1,0:T(8,128)S(1)} %collective-permute-done.29, f32[16,1024]{1,0:T(8,128)S(1)} %collective-permute-done.28, f32[16,1024]{1,0:T(8,128)S(1)} %collective-permute-done.27, ...), dimensions={0} | concatenate | bytes 4292608
  1393.5 303.3 %reduce-scatter.22.cloned.1.call-done = f32[4,24,512]{2,1,0:T(8,128)} async-done(((f32[4,1536,512]{2,1,0:T(8,128)}), f32[4,24,512]{2,1,0:T(8,128)}) %reduce-scatter.22.cloned.1.call-update) | async-done | bytes 196624 | tf_op jit(solution)/shard_map/reduce_scatter | solution.py:420
  1696.8 306.7 %reduce-scatter.18.cloned.1.call-done = f32[4,8,1536]{2,1,0:T(8,128)} async-done(((f32[4,512,1536]{2,1,0:T(8,128)}), f32[4,8,1536]{2,1,0:T(8,128)}) %reduce-scatter.18.cloned.1.call-update) | async-done | bytes 196624 | tf_op jit(solution)/shard_map/reduce_scatter | solution.py:418
  2003.5 306.3 %reduce-scatter.16.cloned.1.call-done = f32[4,24,512]{2,1,0:T(8,128)} async-done(((f32[4,1536,512]{2,1,0:T(8,128)}), f32[4,24,512]{2,1,0:T(8,128)}) %reduce-scatter.16.cloned.1.call-update) | async-done | bytes 196624 | tf_op jit(solution)/shard_map/reduce_scatter | solution.py:417
  (539 shorter events, 596.3 us)
Async XLA Ops:
  61.7 92.9 %all-to-all-start = ((bf16[8,120,1536]{2,1,0:T(8,128)(2,1)}), bf16[8,120,1536]{2,1,0:T(8,128)(2,1)}, u32[]{:S(2)}, u32[]{:S(2)}) async-start(bf16[8,120,1536]{2,1,0:T(8,128)(2,1)} %bitcast.278), calls=%async_computation | async-start | bytes 5898240 | tf_op jit(solution)/shard_map/all_to_all | solution.py:145
  199.8 38.7 %all-to-all-start.1 = ((bf16[8,120,1536]{2,1,0:T(8,128)(2,1)}), bf16[8,120,1536]{2,1,0:T(8,128)(2,1)}, u32[]{:S(2)}, u32[]{:S(2)}) async-start(bf16[8,120,1536]{2,1,0:T(8,128)(2,1)} %bitcast.285), calls=%async_computation.1 | async-start | bytes 5898240 | tf_op jit(solution)/shard_map/all_to_all | solution.py:192
  337.5 36.8 %all-to-all-start.3 = ((bf16[8,120,1536]{2,1,0:T(8,128)(2,1)}), bf16[8,120,1536]{2,1,0:T(8,128)(2,1)}, u32[]{:S(2)}, u32[]{:S(2)}) async-start(bf16[8,120,1536]{2,1,0:T(8,128)(2,1)} %bitcast.286), calls=%async_computation.3 | async-start | bytes 5898240 | tf_op jit(solution)/shard_map/all_to_all | solution.py:224
  458.6 35.3 %all-to-all-start.5 = ((bf16[8,120,1536]{2,1,0:T(8,128)(2,1)}), bf16[8,120,1536]{2,1,0:T(8,128)(2,1)}, u32[]{:S(2)}, u32[]{:S(2)}) async-start(bf16[8,120,1536]{2,1,0:T(8,128)(2,1)} %bitcast.287), calls=%async_computation.5 | async-start | bytes 5898240 | tf_op jit(solution)/shard_map/all_to_all | solution.py:283
  587.7 34.1 %all-to-all-start.6 = ((bf16[8,120,1536]{2,1,0:T(8,128)(2,1)}), bf16[8,120,1536]{2,1,0:T(8,128)(2,1)}, u32[]{:S(2)}, u32[]{:S(2)}) async-start(bf16[8,120,1536]{2,1,0:T(8,128)(2,1)} %bitcast.279), calls=%async_computation.6 | async-start | bytes 5898240 | tf_op jit(solution)/shard_map/all_to_all | solution.py:319
  593.0 158.6 %reduce-scatter.26.cloned.1.call-start = ((), (), s32[]{:S(2)}) async-start(), calls=%async_computation.20 | async-start | bytes 1179648
  678.5 40.8 %all-to-all-start.7 = ((bf16[8,120,1536]{2,1,0:T(8,128)(2,1)}), bf16[8,120,1536]{2,1,0:T(8,128)(2,1)}, u32[]{:S(2)}, u32[]{:S(2)}) async-start(bf16[8,120,1536]{2,1,0:T(8,128)(2,1)} %bitcast.284), calls=%async_computation.7 | async-start | bytes 5898240 | tf_op jit(solution)/shard_map/all_to_all | solution.py:359
  683.9 70.1 %reduce-scatter.28.cloned.1.call-start = ((), (), s32[]{:S(2)}) async-start(), calls=%async_computation.21 | async-start | bytes 1179648
  700.4 619.3 %all-reduce.17.cloned.1.call-start = ((), (), s32[]{:S(2)}) async-start(), calls=%async_computation.22 | async-start | bytes 229376
  762.2 631.3 %reduce-scatter.24.cloned.1.call-start = ((), (), s32[]{:S(2)}) async-start(), calls=%async_computation.19 | async-start | bytes 12779520 | tf_op jit(solution)/shard_map/reduce_scatter | solution.py:421
  770.9 622.5 %reduce-scatter.20.cloned.1.call-start = ((), (), s32[]{:S(2)}) async-start(), calls=%async_computation.17 | async-start | bytes 12779520 | tf_op jit(solution)/shard_map/reduce_scatter | solution.py:419
  779.5 917.3 %reduce-scatter.22.cloned.1.call-start = ((), (), s32[]{:S(2)}) async-start(), calls=%async_computation.18 | async-start | bytes 12779520 | tf_op jit(solution)/shard_map/reduce_scatter | solution.py:420
  788.2 1215.3 %reduce-scatter.18.cloned.1.call-start = ((), (), s32[]{:S(2)}) async-start(), calls=%async_computation.16 | async-start | bytes 12779520 | tf_op jit(solution)/shard_map/reduce_scatter | solution.py:418
  796.8 1513.0 %reduce-scatter.16.cloned.1.call-start = ((), (), s32[]{:S(2)}) async-start(), calls=%async_computation.15 | async-start | bytes 12779520 | tf_op jit(solution)/shard_map/reduce_scatter | solution.py:417
  1235.2 18.5 collective-permute-start.30
  1255.0 18.0 collective-permute-start.24
  1256.4 18.7 collective-permute-start.23
  1257.7 20.5 collective-permute-start.22
  1300.4 21.9 collective-permute-start.9
  1304.4 20.9 collective-permute-start.8
  1307.0 20.1 collective-permute-start.7
  1309.0 21.5 collective-permute-start.6
  1313.3 21.7 collective-permute-start.5
  1322.2 17.1 collective-permute-start.4
  (127 other events, 2527.5 us)
Sparse Core Ops, SparseCore 0:
  665.5 29.2 reduce-scatter.25
  700.5 32.6 reduce-scatter.27
  762.3 158.6 all-reduce.16
Sparse Core Ops, SparseCore 1:
  771.0 311.1 reduce-scatter.23
  1085.2 305.9 reduce-scatter.19
  1394.1 302.6 reduce-scatter.21
  1699.9 303.5 reduce-scatter.17
  2006.6 303.1 reduce-scatter.15
where the time goes:
time: 2330 us; the launch traced here: 2320 us
  waiting for transfers between devices  1030 us (44%)
  blocking collectives  518 us (22%)
  local copies, waits for them, and re-layouts  338 us (15%)
  matrix products  147 us (6%)
  other arithmetic  136 us (6%)
  starting transfers between devices  128 us (5%)
    unnamed x1, blocking collectives  424 us
    reduce_scatter x1, waiting for transfers between devices, per_device(): lax.psum_scatter(grad_out, 'dp', scatter_dimension=1, tiled=True)  307 us
    reduce_scatter x1, waiting for transfers between devices, per_device(): lax.psum_scatter(grad_query, 'dp', scatter_dimension=1, tiled=True)  306 us
    reduce_scatter x1, waiting for transfers between devices, per_device(): lax.psum_scatter(grad_up, 'dp', scatter_dimension=1, tiled=True)  303 us
    unnamed x35, starting transfers between devices  94.6 us
    unnamed x227, local copies, waits for them, and re-layouts  91.6 us
    gather x8, local copies, waits for them, and re-layouts, gather_rows(): return jnp.take(padded, row_index, axis=0)  69.3 us
  transfers between devices with their start and end apart: 46, of which 9 were waited for; matrix products, arithmetic and copies ran while one was open for 30% of the time, Pallas kernels for 0%

commit v1 on v0

v1 whole, which is shorter than its diff:
```python
from functools import partial
import math

import jax
import jax.numpy as jnp
from jax import lax
from jax.experimental import pallas as pl
from jax.experimental.pallas import tpu as pltpu
from jax.sharding import Mesh, PartitionSpec as P

D = 1536
HD = 64
KVH = 8
FF = 512
QW = 512
NSEG = 13
TOK = 384
CAP = 120
PAD = 128
PAIRS = 2 * TOK
EPS = 1e-06
MIB = 1 << 20
F32 = jnp.float32
BF16 = jnp.bfloat16
I32 = jnp.int32

NT = (((1,), (1,)), ((), ()))
NN = (((1,), (0,)), ((), ()))
TN = (((0,), (0,)), ((), ()))


def mm(a, b, dims=NN):
    return lax.dot_general(a, b, dims, preferred_element_type=F32)


def iota(shape, dim):
    return lax.broadcasted_iota(I32, shape, dim)


def params(mib):
    return pltpu.CompilerParams(vmem_limit_bytes=mib * MIB)


VSPEC = pl.BlockSpec(memory_space=pltpu.VMEM)
SSPEC = pl.BlockSpec(memory_space=pltpu.SMEM)
ANY = pl.BlockSpec(memory_space=pl.ANY)


def make_meta(tree, len_ref, par_ref, order_ref, routes, out_ref):
    token = iota((PAIRS, TOK), 1)
    eye = iota((PAIRS, PAIRS), 0) == iota((PAIRS, PAIRS), 1)
    lane = iota((PAIRS, PAD), 1)
    tri = (iota((PAIRS, PAIRS), 0) > iota((PAIRS, PAIRS), 1)).astype(F32).astype(BF16)
    for sub in range(2):
        order = order_ref[0, tree, sub : sub + 1].astype(F32)
        order = jnp.sum(jnp.where(eye, order, 0.0), axis=1, keepdims=True).astype(I32)
        hit = [order == 2 * token + k for k in range(2)]
        named = routes[sub][0, tree].astype(F32)
        expert = jnp.zeros((PAIRS, 1), F32)
        for k in range(2):
            expert = expert + jnp.sum(
                jnp.where(hit[k], named[k : k + 1], 0.0), axis=1, keepdims=True
            )
        onehot = (expert == lane.astype(F32)).astype(F32)
        earlier = mm(tri, onehot.astype(BF16))
        rank = jnp.sum(earlier * onehot, axis=1, keepdims=True)
        code = expert * 1024.0 + rank
        for k in range(2):
            row = jnp.sum(jnp.where(hit[k], code, 0.0), axis=0, keepdims=True)
            out_ref[2 * sub + k : 2 * sub + k + 1] = row.astype(I32)

    def segments(place):
        seg = jnp.full(place.shape, -1, I32)
        start = jnp.int32(0)
        for s in range(NSEG):
            seg = seg + (place >= start).astype(I32)
            start = start + len_ref[0, tree, s]
        parent = jnp.zeros(place.shape, I32)
        for s in range(NSEG):
            parent = jnp.where(seg == s, par_ref[0, tree, s], parent)
        grand = jnp.zeros(place.shape, I32)
        for s in range(NSEG):
            grand = jnp.where(parent == s, par_ref[0, tree, s], grand)
        return seg, parent, grand

    seg, parent, grand = segments(iota((1, TOK), 1))
    key_seg, _, _ = segments(iota((TOK, 1), 0))
    allowed = ((key_seg == seg) | (key_seg == parent) | (key_seg == grand)) & (
        iota((TOK, TOK), 0) <= iota((TOK, TOK), 1)
    )
    depth = jnp.sum(allowed.astype(F32), axis=0, keepdims=True) - 1.0
    out_ref[4:5] = seg
    out_ref[5:6] = parent
    out_ref[6:7] = grand
    out_ref[7:8] = depth.astype(I32)


def sine_cosine(angle):
    turns = jnp.floor(angle * (2.0 / math.pi) + 0.5)
    rest = (angle - turns * 1.5703125) - turns * 4.838267948966e-4
    square = rest * rest
    sine = rest + rest * square * (
        -1.6666654611e-1 + square * (8.3321608736e-3 + square * -1.9515295891e-4)
    )
    cosine = (1.0 - 0.5 * square) + square * square * (
        4.166664568298827e-2 + square * (-1.388731625493765e-3 + square * 2.443315711809948e-5)
    )
    quarter = turns.astype(I32) & 3
    odd = (quarter & 1) == 1
    first, second = jnp.where(odd, cosine, sine), jnp.where(odd, sine, cosine)
    first = jnp.where(quarter >= 2, -first, first)
    second = jnp.where((quarter == 1) | (quarter == 2), -second, second)
    return first, second


def turn(values, place, sign):
    rows = values.shape[0]
    lane = iota((1, 128), 1)
    frequency = jnp.exp((lane % 32).astype(F32) * (-math.log(10000.0) / 32.0))
    angle = place * frequency
    sine, cosine = sine_cosine(angle)
    sine = sine * sign
    first = (iota((rows, 128), 1) % 64) < 32
    sine = jnp.where(first, -sine, sine)
    parts = []
    for b in range(QW // 128):
        v = values[:, 128 * b : 128 * b + 128]
        other = jnp.where(first, pltpu.roll(v, 96, 1), pltpu.roll(v, 32, 1))
        parts.append(v * cosine + other * sine)
    return jnp.concatenate(parts, axis=1)


def as_column(row):
    eye = iota((TOK, TOK), 0) == iota((TOK, TOK), 1)
    return jnp.sum(jnp.where(eye, row, 0.0), axis=1, keepdims=True)


def hits(meta, sub, expert):
    slot = iota((PAD, 1), 0)
    target = jnp.where(slot < CAP, expert * 1024 + slot, -1)
    return (meta[2 * sub : 2 * sub + 1] == target), (meta[2 * sub + 1 : 2 * sub + 2] == target)


def places(meta, sub, base):
    both = []
    for e in range(2):
        first, second = hits(meta, sub, base + e)
        both.append((first | second).astype(F32))
    return jnp.concatenate(both, axis=0).astype(BF16)


def weighted_places(meta, gates, sub, base):
    both = []
    for e in range(2):
        first, second = hits(meta, sub, base + e)
        both.append(jnp.where(first, gates[0:1], 0.0) + jnp.where(second, gates[1:2], 0.0))
    return jnp.concatenate(both, axis=0).astype(BF16)


def slot_gate(meta, gates, sub, expert):
    first, second = hits(meta, sub, expert)
    weighted = jnp.where(first, gates[0:1], 0.0) + jnp.where(second, gates[1:2], 0.0)
    return jnp.sum(weighted, axis=1, keepdims=True)


def token_sums(meta, sub, expert, column):
    first, second = hits(meta, sub, expert)
    return jnp.concatenate(
        [
            jnp.sum(jnp.where(first, column, 0.0), axis=0, keepdims=True),
            jnp.sum(jnp.where(second, column, 0.0), axis=0, keepdims=True),
        ],
        axis=0,
    )


def pair_gates(meta, sub, logits):
    row = iota((8, TOK), 0)
    picked = [
        jnp.sum(
            jnp.where(row == meta[2 * sub + k : 2 * sub + k + 1] // 1024, logits, 0.0),
            axis=0,
            keepdims=True,
        )
        for k in range(2)
    ]
    top = jnp.maximum(picked[0], picked[1])
    raised = [jnp.exp(p - top) for p in picked]
    total = raised[0] + raised[1]
    return jnp.concatenate([raised[0] / total, raised[1] / total], axis=0)


def slot_depth(meta, expert):
    first, second = hits(meta, 0, expert)
    return jnp.sum(jnp.where(first | second, meta[7:8].astype(F32), 0.0), axis=1, keepdims=True)


def slot_mask(columns, expert):
    slot = iota((1, PAD), 1)
    target = jnp.where(slot < CAP, expert * 1024 + slot, -1).astype(F32)
    hit = (columns[:, 0:1] == target) | (columns[:, 1:2] == target)

    def row(column):
        return jnp.sum(jnp.where(hit, column, 0.0), axis=0, keepdims=True)

    key = iota((TOK, 1), 0).astype(F32)
    seg = columns[:, 4:5]
    return (
        (seg == row(seg)) | (seg == row(columns[:, 5:6])) | (seg == row(columns[:, 6:7]))
    ) & (key <= row(key))


def two_heads(rows, masks):
    return jnp.concatenate([rows * masks[0], rows * masks[1]], axis=0)


def softmax_keys(scores, allowed):
    probs = []
    for h in range(2):
        one = jnp.where(allowed, scores[:, PAD * h : PAD * h + PAD] * HD ** (-0.5), -1e30)
        raised = jnp.exp(one - jnp.max(one, axis=0, keepdims=True))
        probs.append(raised * (1.0 / jnp.sum(raised, axis=0, keepdims=True)))
    return probs


def own_lanes(both):
    return jnp.concatenate([both[0:64, 0:PAD], both[64:128, PAD:]], axis=0).T


def logit_grads(meta, sub, gates, grads):
    inner = gates[0:1] * grads[0:1] + gates[1:2] * grads[1:2]
    row = iota((8, TOK), 0)
    total = jnp.zeros((8, TOK), F32)
    for k in range(2):
        picked = gates[k : k + 1] * (grads[k : k + 1] - inner)
        total = total + jnp.where(
            row == meta[2 * sub + k : 2 * sub + k + 1] // 1024, picked, 0.0
        )
    return total.astype(BF16)


def head_masks():
    lane = iota((1, 128), 1)
    return (lane < 64).astype(F32).astype(BF16), (lane >= 64).astype(F32).astype(BF16)


def fetch(pairs, sems):
    copies = []
    for n, (source, target) in enumerate(pairs):
        copy = pltpu.make_async_copy(source, target, sems.at[n])
        copy.start()
        copies.append(copy)
    return copies


MESH = pl.DeviceIdType.MESH
CH = 128
CHUNKS = TOK // CH


class Link:
    def __init__(self, send, recv):
        self.send, self.recv, self.count = send, recv, 0

    def copy(self, source, target, device):
        n = self.count
        self.count += 1
        copy = pltpu.make_async_remote_copy(
            src_ref=source,
            dst_ref=target,
            send_sem=self.send.at[n],
            recv_sem=self.recv.at[n],
            device_id=device,
            device_id_type=MESH,
        )
        copy.start()
        return copy


def around(axes):
    devices = []
    for axis in axes:
        n = lax.axis_size(axis)
        if n > 1:
            me = lax.axis_index(axis)
            devices += [{axis: lax.rem(me + 1, n)}, {axis: lax.rem(me + n - 1, n)}]
    return devices


def flip(*axes):
    return {axis: 1 - lax.axis_index(axis) for axis in axes}


def first_expert():
    local = 2 * lax.axis_index("c")
    return 4 * lax.axis_index("zh") + local, local


def greet(devices):
    barrier = pltpu.get_barrier_semaphore()
    for device in devices:
        pl.semaphore_signal(barrier, inc=1, device_id=device, device_id_type=MESH)
    pl.semaphore_wait(barrier, len(devices))


def part(j):
    return slice(CH * j, CH * j + CH)


class Collect:
    def __init__(self, link, own, mate, far, far_mate, abuf, bbuf, fbuf, rbuf):
        self.link, self.fbuf, self.rbuf, self.abuf, self.bbuf = link, fbuf, rbuf, abuf, bbuf
        self.own, self.mate, self.far, self.far_mate = own, mate, far, far_mate

    def send_far_mate(self):
        self.a = [
            self.link.copy(self.far_mate.at[part(j)], self.abuf.at[part(j)], flip("c"))
            for j in range(CHUNKS)
        ]

    def send_mate(self):
        self.b = [
            self.link.copy(self.mate.at[part(j)], self.bbuf.at[part(j)], flip("c"))
            for j in range(CHUNKS)
        ]

    def forward(self):
        self.f = []
        for j in range(CHUNKS):
            self.a[j].wait_recv()
            total = self.far[part(j)].astype(F32) + self.abuf[part(j)].astype(F32)
            self.fbuf[part(j)] = total.astype(BF16)
            self.f.append(
                self.link.copy(self.fbuf.at[part(j)], self.rbuf.at[part(j)], flip("zl", "zh"))
            )

    def total(self, j):
        self.b[j].wait_recv()
        self.f[j].wait_recv()
        return (
            self.own[part(j)].astype(F32)
            + self.bbuf[part(j)].astype(F32)
            + self.rbuf[part(j)].astype(F32)
        )

    def close(self):
        for copy in self.a + self.b + self.f:
            copy.wait_send()


class Spread:
    def __init__(self, link, own, landed, target, sems):
        self.link, self.own, self.landed, self.target, self.sems = link, own, landed, target, sems
        self.far, self.mate, self.local, self.relayed = [], [], [], []

    def keep(self, source, tree, j):
        local = pltpu.make_async_copy(
            source, self.target.at[tree, part(j)], self.sems.at[len(self.local)]
        )
        local.start()
        self.local.append(local)

    def send(self, j):
        source = self.own.at[part(j)]
        self.far.append(self.link.copy(source, self.landed.at[part(j)], flip("zl", "zh")))
        self.mate.append(self.link.copy(source, self.target.at[1, part(j)], flip("c")))
        self.keep(source, 0, j)

    def relay(self, j):
        self.far[j].wait_recv()
        source = self.landed.at[part(j)]
        self.relayed.append(self.link.copy(source, self.target.at[3, part(j)], flip("c")))
        self.keep(source, 2, j)

    def close(self):
        for copy in self.mate + self.relayed:
            copy.wait_recv()
        for copy in self.far + self.mate + self.relayed:
            copy.wait_send()
        for copy in self.local:
            copy.wait()


class Pairs:
    def __init__(self, link, keep, give, buf, mid, far):
        self.link, self.keep, self.buf, self.mid, self.far = link, keep, buf, mid, far
        self.first = link.copy(give, buf, flip("c"))

    def forward(self):
        self.first.wait_recv()
        self.mid[...] = self.keep[1] + self.buf[1]
        self.second = self.link.copy(self.mid, self.far, flip("zl", "zh"))

    def total(self):
        self.second.wait_recv()
        return self.keep[0] + self.buf[0] + self.far[...]

    def close(self):
        self.first.wait_send()
        self.second.wait_send()


class Ring:
    def __init__(self, link, axis, view, buf0, buf1):
        self.link, self.axis, self.view, self.buf0, self.buf1 = link, axis, view, buf0, buf1
        self.n = lax.axis_size(axis)
        me = lax.axis_index(axis)
        self.at = lambda step: lax.rem(me + step + self.n, self.n)

    def start(self):
        if self.n == 1:
            return
        right, left = {self.axis: self.at(1)}, {self.axis: self.at(-1)}
        self.c0 = self.link.copy(self.view(self.at(2), 0), self.buf0.at[0], right)
        self.c1 = self.link.copy(self.view(self.at(2), 1), self.buf1.at[0], left)
        self.c2 = self.link.copy(self.view(self.at(1), 1), self.buf1.at[1], right)
        self.c3 = self.link.copy(self.view(self.at(-1), 0), self.buf0.at[2], left)

    def middle(self):
        if self.n == 1:
            return
        right, left = {self.axis: self.at(1)}, {self.axis: self.at(-1)}
        self.c0.wait_recv()
        held = self.view(self.at(1), 0)
        held[...] = (held[...].astype(F32) + self.buf0[0].astype(F32)).astype(BF16)
        self.c4 = self.link.copy(held, self.buf0.at[1], right)
        self.c1.wait_recv()
        held = self.view(self.at(-1), 1)
        held[...] = (held[...].astype(F32) + self.buf1[0].astype(F32)).astype(BF16)
        self.c5 = self.link.copy(held, self.buf1.at[2], left)

    def end(self, store):
        if self.n == 1:
            for h in range(2):
                store(h, self.view(0, h)[...].astype(F32))
            return
        for h, waits, buf in ((0, (self.c4, self.c3), self.buf0), (1, (self.c2, self.c5), self.buf1)):
            for copy in waits:
                copy.wait_recv()
            store(
                h,
                self.view(self.at(0), h)[...].astype(F32) + buf[1].astype(F32) + buf[2].astype(F32),
            )

    def close(self):
        if self.n > 1:
            for copy in (self.c0, self.c1, self.c2, self.c3, self.c4, self.c5):
                copy.wait_send()


def split(rows):
    first = (rows // 2 + 15) // 16 * 16
    return slice(0, first), slice(first, rows)


def ring_buffers(lead, rows):
    return [pltpu.VMEM((3,) + lead + (s.stop - s.start, 512), BF16) for s in split(rows)]


def remote_params(mib, ident):
    return pltpu.CompilerParams(
        vmem_limit_bytes=mib * MIB, collective_id=ident, has_side_effects=True
    )


ROWS_BUF = pltpu.VMEM((TOK, D), BF16)


class Gather:
    def __init__(self, link, source, target):
        self.link, self.source, self.target = link, source, target

    def send(self):
        self.far = [
            self.link.copy(self.source.at[part(j)], self.target.at[1, part(j)], flip("zl", "zh"))
            for j in range(CHUNKS)
        ]
        self.mate = self.link.copy(self.source, self.target.at[0], flip("c"))
        self.relayed = []

    def relay(self, j):
        self.far[j].wait_recv()
        self.relayed.append(
            self.link.copy(self.target.at[1, part(j)], self.target.at[2, part(j)], flip("c"))
        )

    def close(self):
        for copy in self.far + [self.mate] + self.relayed:
            copy.wait_send()


def forward_kernel(*refs):
    (
        len_ref, par_ref, order_ref, routes_one, routes_two, x_ref, gain_ref, gain_two_ref, router_ref,
        cot_ref, kv_hbm, wq_hbm, wo_hbm,
        n_hbm, k_hbm, v_hbm, r_hbm, q_hbm, a_hbm, n2_hbm, cots_hbm, gate_ref, meta_ref, middle_ref,
        xb, nb, kb, vb, vt, columns, rb, qb, ab, obuf, pb, kv, wq, wo, mbuf, abuf, bbuf, fbuf, rbuf, own,
        landed, cb, wsem, osem, sems, ssem, rsem,
    ) = refs
    base, local = first_expert()
    link = Link(ssem, rsem)
    load = fetch(
        [(kv_hbm, kv), (wq_hbm.at[pl.ds(local, 2)], wq), (wo_hbm.at[pl.ds(local, 2)], wo)], wsem
    )
    saved = []

    def save(source, target):
        copy = pltpu.make_async_copy(source, target, osem.at[len(saved)])
        copy.start()
        saved.append(copy)

    far, mate = flip("zl", "zh"), flip("c")
    greet([mate, far])
    inputs = Gather(link, x_ref, xb)
    cots = Gather(link, cot_ref, cb)
    collect = Collect(link, pb.at[0], pb.at[1], pb.at[2], pb.at[3], abuf, bbuf, fbuf, rbuf)
    spread = Spread(link, own, landed, n2_hbm, sems)
    inputs.send()
    make_meta(
        lax.axis_index("zh"), len_ref, par_ref, order_ref, (routes_one, routes_two), mbuf.at[0]
    )
    meta_far = link.copy(mbuf.at[0], mbuf.at[2], far)
    meta_mate = link.copy(mbuf.at[0], mbuf.at[1], mate)
    gate_ref[...] = jnp.zeros_like(gate_ref)

    def tree(s, source):
        meta = mbuf[s]
        x = source[...].astype(F32)
        inverse = lax.rsqrt(jnp.mean(x * x, axis=-1, keepdims=True) + EPS)
        normed = (x * inverse * gain_ref[...].reshape(1, D)).astype(BF16)
        nb[s] = normed
        save(nb.at[s], n_hbm.at[s])
        depth = as_column(meta[7:8].astype(F32))
        kb[s] = turn(mm(normed, kv[:, :QW]), depth, 1.0).astype(BF16)
        save(kb.at[s], k_hbm.at[s])
        value = mm(normed, kv[:, QW:])
        vb[s] = value.astype(BF16)
        save(vb.at[s], v_hbm.at[s])
        vt[s] = value.T.astype(BF16)
        columns[s] = meta.astype(F32).T
        moved = mm(places(meta, 0, base), normed).astype(BF16)
        for e in range(2):
            rb[e, PAD * s : PAD * s + PAD] = moved[PAD * e : PAD * e + PAD]
            save(rb.at[e, pl.ds(PAD * s, PAD)], r_hbm.at[e, pl.ds(PAD * s, PAD)])
        gate_ref[s, 0:2] = pair_gates(meta, 0, mm(router_ref[...], normed, NT))

    masks = head_masks()

    def attend(first, between=None):
        group = slice(PAD * first, PAD * first + 2 * PAD)
        for e in range(2):
            depth = jnp.concatenate(
                [slot_depth(mbuf[first + n], base + e) for n in range(2)], axis=0
            )
            qb[e, group] = turn(mm(rb[e, group], wq[e]), depth, 1.0).astype(BF16)

        def block(n, carry):
            e, s = n // 2, first + n % 2
            allowed = slot_mask(columns[s], base + e)
            start = pl.multiple_of(s * PAD, PAD)
            for pair in range(4):
                cols = slice(128 * pair, 128 * pair + 128)
                q = two_heads(qb[e, pl.ds(start, PAD), cols], masks)
                probs = softmax_keys(mm(kb[s, :, cols], q, NT), allowed)
                probs = jnp.concatenate([p.astype(BF16) for p in probs], axis=1)
                ab[e, pl.ds(start, PAD), cols] = own_lanes(mm(vt[s, cols], probs)).astype(BF16)
            return carry

        lax.fori_loop(0, 4, block, 0)
        if between is not None:
            between()
        for e in range(2):
            save(qb.at[e, pl.ds(PAD * first, 2 * PAD)], q_hbm.at[e, pl.ds(PAD * first, 2 * PAD)])
            save(ab.at[e, pl.ds(PAD * first, 2 * PAD)], a_hbm.at[e, pl.ds(PAD * first, 2 * PAD)])
            obuf[e] = mm(ab[e, group], wo[e]).astype(BF16)
        for n in (1, 0):
            s = first + n
            pb[s] = mm(
                weighted_places(mbuf[s], gate_ref[s], 0, base),
                jnp.concatenate([obuf[e, PAD * n : PAD * n + PAD] for e in range(2)], axis=0),
                TN,
            ).astype(BF16)
            if s == 3:
                collect.send_far_mate()
            if s == 1:
                collect.send_mate()

    load[0].wait()
    tree(0, x_ref)
    meta_far.wait_recv()
    meta_on = link.copy(mbuf.at[2], mbuf.at[3], mate)
    meta_mate.wait_recv()
    inputs.relay(0)
    inputs.mate.wait_recv()
    tree(1, xb.at[0])
    load[1].wait()
    load[2].wait()
    attend(0, lambda: inputs.relay(1))
    inputs.relay(2)
    cots.send()
    tree(2, xb.at[1])
    for copy in inputs.relayed:
        copy.wait_recv()
    meta_on.wait_recv()
    tree(3, xb.at[2])
    attend(2)
    meta_ref[...] = mbuf[...]
    collect.forward()
    for j in range(CHUNKS):
        middle = x_ref[part(j)].astype(F32) + collect.total(j)
        middle_ref[part(j)] = middle
        inverse = lax.rsqrt(jnp.mean(middle * middle, axis=-1, keepdims=True) + EPS)
        own[part(j)] = (middle * inverse * gain_two_ref[...].reshape(1, D)).astype(BF16)
        spread.send(j)
    for j in range(CHUNKS):
        cots.relay(j)
    cots.mate.wait_recv()
    save(cb.at[pl.ds(0, 2)], cots_hbm.at[pl.ds(0, 2)])
    for j in range(CHUNKS):
        spread.relay(j)
    for copy in cots.relayed:
        copy.wait_recv()
    save(cb.at[2], cots_hbm.at[2])
    for copy in (meta_far, meta_mate, meta_on):
        copy.wait_send()
    inputs.close()
    cots.close()
    collect.close()
    spread.close()
    for copy in saved:
        copy.wait()


def forward_call(*operands):
    rows = jax.ShapeDtypeStruct((4, TOK, D), BF16)
    heads = jax.ShapeDtypeStruct((4, TOK, QW), BF16)
    slots = jax.ShapeDtypeStruct((2, 4 * PAD, QW), BF16)
    copies = 2 * (2 * CHUNKS + 1) + 3 + 6 * CHUNKS
    return pl.pallas_call(
        forward_kernel,
        out_shape=(
            rows,
            heads,
            heads,
            jax.ShapeDtypeStruct((2, 4 * PAD, D), BF16),
            slots,
            slots,
            rows,
            jax.ShapeDtypeStruct((3, TOK, D), BF16),
            jax.ShapeDtypeStruct((4, 8, TOK), F32),
            jax.ShapeDtypeStruct((4, 8, TOK), I32),
            jax.ShapeDtypeStruct((TOK, D), F32),
        ),
        in_specs=[SSPEC] * 2 + [VSPEC] * 8 + [ANY] * 3,
        out_specs=(ANY,) * 8 + (VSPEC,) * 3,
        scratch_shapes=[
            pltpu.VMEM((3, TOK, D), BF16),
            pltpu.VMEM((4, TOK, D), BF16),
            pltpu.VMEM((4, TOK, QW), BF16),
            pltpu.VMEM((4, TOK, QW), BF16),
            pltpu.VMEM((4, QW, TOK), BF16),
            pltpu.VMEM((4, TOK, 8), F32),
            pltpu.VMEM((2, 4 * PAD, D), BF16),
            pltpu.VMEM((2, 4 * PAD, QW), BF16),
            pltpu.VMEM((2, 4 * PAD, QW), BF16),
            pltpu.VMEM((2, 2 * PAD, D), BF16),
            pltpu.VMEM((4, TOK, D), BF16),
            pltpu.VMEM((D, 2 * QW), BF16),
            pltpu.VMEM((2, D, QW), BF16),
            pltpu.VMEM((2, QW, D), BF16),
            pltpu.VMEM((4, 8, TOK), I32),
        ]
        + [ROWS_BUF] * 6
        + [
            pltpu.VMEM((3, TOK, D), BF16),
            pltpu.SemaphoreType.DMA((3,)),
            pltpu.SemaphoreType.DMA((30,)),
            pltpu.SemaphoreType.DMA((2 * CHUNKS,)),
            pltpu.SemaphoreType.DMA((copies,)),
            pltpu.SemaphoreType.DMA((copies,)),
        ],
        compiler_params=remote_params(60, 1),
        cost_estimate=pl.CostEstimate(flops=10**9, bytes_accessed=300 * 10**6, transcendentals=0),
        name="attention_forward",
    )(*operands)


def expert_block(nx, ny):
    return D // (nx * ny), FF // (nx * ny)


def mlp_kernel(nx, ny, *refs):
    (
        mbuf, router_ref, gain_ref, n4_hbm, cot_hbm, cots_hbm, middle_hbm, wg_hbm, wu_hbm, wd_hbm,
        dm_ref, gain_grad_ref, router_grad_ref, sa_ref, sb_ref, dm4_ref, keep_out, give_out,
    ) = refs[:18]
    (
        pbuf, gb, mr, gr, dgu, hg, obuf, dbuf, big, middle, cot, normed, own, landed, abuf, bbuf, fbuf, rbuf,
        gates, dgk, dgg, gpair, gmid, gfar, a0, a1, b0, b1, c0, c1, d0, d1, sems, lsem, osem, ssem, rsem,
    ) = refs[18:]
    base, local = first_expert()
    r, rq = expert_block(nx, ny)
    half = (2 * r + 3 * rq) // 2
    halves = split(half)
    link = Link(ssem, rsem)
    load = fetch(
        [(n4_hbm.at[pl.ds(2, 2)], pbuf.at[pl.ds(2, 2)]), (cots_hbm.at[pl.ds(1, 2)], gb.at[pl.ds(2, 2)])]
        + [(wg_hbm.at[pl.ds(local, 2)], big.at[:, :, :, 0:r])]
        + [(wu_hbm.at[pl.ds(local, 2)], big.at[:, :, :, r : 2 * r])]
        + [
            (
                wd_hbm.at[pl.ds(local, 2), :, :, :, pl.ds(512 * k, 512)],
                big.at[:, :, :, 2 * r + rq * k : 2 * r + rq * k + rq],
            )
            for k in range(3)
        ]
        + [(n4_hbm.at[pl.ds(0, 2)], pbuf.at[pl.ds(0, 2)])]
        + [(cot_hbm, gb.at[0]), (cots_hbm.at[0], gb.at[1])]
        + [(n4_hbm.at[0], normed), (cot_hbm, cot), (middle_hbm, middle)],
        lsem,
    )
    greet([flip("c"), flip("zl", "zh")] + around(("x", "y")))
    dgk[...] = jnp.zeros_like(dgk)
    dgg[...] = jnp.zeros_like(dgg)
    collect = Collect(
        link, pbuf.at[0], pbuf.at[1], pbuf.at[2], pbuf.at[3], abuf, bbuf, fbuf, rbuf
    )
    spread = Spread(link, own, landed, dm4_ref, sems)
    saved = []

    def save(source, target):
        copy = pltpu.make_async_copy(source, target, osem.at[len(saved)])
        copy.start()
        saved.append(copy)

    def to_slots(s):
        gates[s] = pair_gates(mbuf[s], 1, mm(router_ref[...], pbuf[s], NT))
        hot = places(mbuf[s], 1, base)
        rows = slice(PAD * s, PAD * s + PAD)
        for source, target in ((pbuf, mr), (gb, gr)):
            moved = mm(hot, source[s]).astype(BF16)
            target[0, rows] = moved[:PAD]
            target[1, rows] = moved[PAD:]

    def weight(e, k):
        if k < 2:
            return big[e, :, :, r * k : r * k + r].reshape(D, FF)
        first = 2 * r + rq * (k - 2)
        return big[e, :, :, first : first + rq].reshape(FF, 512)

    def experts(first, e):
        rows = slice(PAD * first, PAD * first + 2 * PAD)
        x, grads = mr[e, rows], gr[e, rows]
        gate_pre, up_pre = mm(x, weight(e, 0)), mm(x, weight(e, 1))
        sigmoid = 1.0 / (1.0 + jnp.exp(-gate_pre))
        silu = gate_pre * sigmoid
        hidden = (silu * up_pre).astype(BF16)
        grad = sum(
            mm(grads[:, 512 * k : 512 * k + 512], weight(e, 2 + k), NT) for k in range(3)
        )
        for k in range(3):
            obuf[e, :, 512 * k : 512 * k + 512] = mm(hidden, weight(e, 2 + k)).astype(BF16)
        hidden = hidden.astype(F32)
        grad_gate = jnp.sum(hidden * grad, axis=1, keepdims=True)
        gate = jnp.concatenate(
            [slot_gate(mbuf[first + n], gates[first + n], 1, base + e) for n in range(2)], axis=0
        )
        for n in range(2):
            s = first + n
            (dgg if s % 2 else dgk)[s // 2, 0:2] += token_sums(
                mbuf[s], 1, base + e, grad_gate[PAD * n : PAD * n + PAD]
            )
        hg[e, rows] = (gate * hidden).astype(BF16)
        grad = gate * grad
        grad_gate_pre = (grad * up_pre * sigmoid * (1.0 + gate_pre * (1.0 - sigmoid))).astype(BF16)
        grad_up_pre = (grad * silu).astype(BF16)
        dgu[e, rows, 0:FF] = grad_gate_pre
        dgu[e, rows, FF:] = grad_up_pre
        dbuf[e] = (
            mm(grad_gate_pre, weight(e, 0), NT) + mm(grad_up_pre, weight(e, 1), NT)
        ).astype(BF16)

    def sums(first):
        for n in (1, 0):
            s = first + n
            pbuf[s] = mm(
                places(mbuf[s], 1, base),
                jnp.concatenate([dbuf[e, PAD * n : PAD * n + PAD] for e in range(2)], axis=0),
                TN,
            ).astype(BF16)
            if s == 3:
                collect.send_far_mate()
            if s == 1:
                collect.send_mate()

    def results(first):
        for n in range(2):
            s = first + n
            gb[s] = mm(
                weighted_places(mbuf[s], gates[s], 1, base),
                jnp.concatenate([obuf[e, PAD * n : PAD * n + PAD] for e in range(2)], axis=0),
                TN,
            ).astype(BF16)
            save(gb.at[s], (give_out if s % 2 else keep_out).at[s // 2])

    for copy in load[:2]:
        copy.wait()
    to_slots(2)
    to_slots(3)
    for copy in load[2:7]:
        copy.wait()
    experts(2, 0)
    experts(2, 1)
    sums(2)
    collect.forward()
    results(2)
    for copy in load[7:10]:
        copy.wait()
    to_slots(0)
    to_slots(1)
    later = [slice(half + s.start, half + s.stop) for s in halves]
    rings = [
        [
            Ring(link, "x", lambda i, h: big.at[0, i, :, halves[h]], a0, a1),
            Ring(link, "y", lambda i, h: big.at[0, :, i, later[h]], b0, b1),
        ],
        [
            Ring(link, "x", lambda i, h: big.at[1, i, :, halves[h]], c0, c1),
            Ring(link, "y", lambda i, h: big.at[1, :, i, later[h]], d0, d1),
        ],
    ]
    wide, narrow = D // nx, FF // nx
    for e in range(2):
        experts(0, e)
        for t in range(nx):
            block = mm(mr[e, :, wide * t : wide * t + wide], dgu[e], TN).astype(BF16)
            for k in range(2):
                big[e, t, :, r * k : r * k + r] = block[:, FF * k : FF * k + FF].reshape(ny, r, FF)
            block = mm(hg[e, :, narrow * t : narrow * t + narrow], gr[e], TN).astype(BF16)
            for k in range(3):
                first = 2 * r + rq * k
                big[e, t, :, first : first + rq] = block[:, 512 * k : 512 * k + 512].reshape(
                    ny, rq, 512
                )
        for ring in rings[e]:
            ring.start()
    sums(0)
    for ring in rings[0]:
        ring.middle()
    pairs = Pairs(link, dgk, dgg, gpair, gmid, gfar)
    results(0)
    pairs.forward()
    for copy in load[10:]:
        copy.wait()
    logits = logit_grads(mbuf[0], 1, gates[0], pairs.total())
    router_grad_ref[...] = mm(logits, normed[...])
    gain_grad_ref[...] = jnp.zeros_like(gain_grad_ref)
    for j in range(CHUNKS):
        if j == 1:
            for ring in rings[1]:
                ring.middle()
        grad = collect.total(j) + mm(logits[:, part(j)], router_ref[...], TN)
        mid = middle[part(j)]
        inverse = lax.rsqrt(jnp.mean(mid * mid, axis=-1, keepdims=True) + EPS)
        gain_grad_ref[...] += jnp.sum(grad * (mid * inverse), axis=0, keepdims=True)
        weighted = grad * gain_ref[...].reshape(1, D)
        inner = jnp.mean(weighted * mid, axis=-1, keepdims=True)
        result = (
            cot[part(j)].astype(F32)
            + inverse * weighted
            - mid * (inverse * inverse * inverse * inner)
        )
        own[part(j)] = result.astype(BF16)
        spread.send(j)
        dm_ref[part(j)] = result
    for j in range(CHUNKS):
        spread.relay(j)
    for e in range(2):
        for ring, out in zip(rings[e], (sa_ref, sb_ref)):
            ring.end(keeper(out.at[e], halves))
            ring.close()
    pairs.close()
    collect.close()
    spread.close()
    for copy in saved:
        copy.wait()


def mlp_call(nx, ny, *operands):
    r, rq = expert_block(nx, ny)
    block = 2 * r + 3 * rq
    copies = 6 * CHUNKS + 2 + 24
    part_shape = jax.ShapeDtypeStruct((2, TOK, D), BF16)
    return pl.pallas_call(
        partial(mlp_kernel, nx, ny),
        out_shape=(
            jax.ShapeDtypeStruct((TOK, D), F32),
            jax.ShapeDtypeStruct((1, D), F32),
            jax.ShapeDtypeStruct((8, D), F32),
            jax.ShapeDtypeStruct((2, ny, block // 2, 512), BF16),
            jax.ShapeDtypeStruct((2, nx, block // 2, 512), BF16),
            jax.ShapeDtypeStruct((4, TOK, D), BF16),
            part_shape,
            part_shape,
        ),
        in_specs=[VSPEC] * 3 + [ANY] * 7,
        out_specs=(VSPEC,) * 5 + (ANY,) * 3,
        scratch_shapes=[
            pltpu.VMEM((4, TOK, D), BF16),
            pltpu.VMEM((4, TOK, D), BF16),
            pltpu.VMEM((2, 4 * PAD, D), BF16),
            pltpu.VMEM((2, 4 * PAD, D), BF16),
            pltpu.VMEM((2, 4 * PAD, 2 * FF), BF16),
            pltpu.VMEM((2, 4 * PAD, FF), BF16),
            pltpu.VMEM((2, 2 * PAD, D), BF16),
            pltpu.VMEM((2, 2 * PAD, D), BF16),
            pltpu.VMEM((2, nx, ny, block, 512), BF16),
            pltpu.VMEM((TOK, D), F32),
        ]
        + [ROWS_BUF] * 8
        + [
            pltpu.VMEM((4, 2, TOK), F32),
            pltpu.VMEM((2, 8, TOK), F32),
            pltpu.VMEM((2, 8, TOK), F32),
            pltpu.VMEM((2, 8, TOK), F32),
            pltpu.VMEM((8, TOK), F32),
            pltpu.VMEM((8, TOK), F32),
        ]
        + (ring_buffers((ny,), block // 2) + ring_buffers((nx,), block // 2)) * 2
        + [
            pltpu.SemaphoreType.DMA((2 * CHUNKS,)),
            pltpu.SemaphoreType.DMA((13,)),
            pltpu.SemaphoreType.DMA((4,)),
            pltpu.SemaphoreType.DMA((copies,)),
            pltpu.SemaphoreType.DMA((copies,)),
        ],
        compiler_params=remote_params(63, 2),
        cost_estimate=pl.CostEstimate(flops=10**9, bytes_accessed=250 * 10**6, transcendentals=0),
        name="feed_forward",
    )(*operands)


def of_half(source, index, first, count, side):
    half = count // 2
    return source[index, pl.ds(pl.multiple_of(first + side * half, 8), half)]


def halves_to_send(fields, zsend, zl):
    for e in range(2):
        offset = 0
        for source, first, count in fields:
            zsend[e, offset : offset + count // 2] = of_half(source, e, first, count, 1 - zl).astype(BF16)
            offset += count // 2


def add_halves(fields, zrecv, y, zl):
    for e in range(2):
        offset = 0
        for source, first, count in fields:
            rows = slice(offset, offset + count // 2)
            y[e, rows] = of_half(source, e, first, count, zl) + zrecv[e, rows].astype(F32)
            offset += count // 2


def quarters_to_send(fields, y, csend, core):
    for e in range(2):
        offset = 0
        for _, _, count in fields:
            csend[e, offset // 2 : offset // 2 + count // 4] = of_half(y, e, offset, count // 2, 1 - core)
            offset += count // 2


def place_quarters(fields, targets, y, crecv, core):
    for e in range(2):
        offset = 0
        for (_, _, count), (target, k) in zip(fields, targets):
            n = count // 4
            columns = slice(None) if k is None else slice(512 * k, 512 * k + 512)
            target[core * 2 + e, :, columns] = of_half(y, e, offset, count // 2, core)
            target[(1 - core) * 2 + e, :, columns] = crecv[e, offset // 2 : offset // 2 + n]
            offset += count // 2


def keeper(target, cut, index=None):
    def store(h, value):
        if index is None:
            target[:, cut[h]] = value.astype(target.dtype)
        else:
            target[index, cut[h]] = value.astype(target.dtype)

    return store


def attn_back_kernel(nx, ny, *refs):
    (
        mbuf, gbuf, router_ref, gain_ref, sa_ref, sb_ref, x_hbm, dm_hbm, n_hbm, grads_hbm,
        k_hbm, v_hbm, q_hbm, a_hbm, wq_hbm, wo_hbm, kv_hbm, r_hbm,
    ) = refs[:18]
    gain_grad_ref, router_grad_ref, dkv_ref, tm, oa_ref, ob_ref, input_grad_hbm = refs[18:25]
    (
        input_grad, pbuf, kbuf, vbuf, kt, qbuf, abuf_, wq, wo, kv, dr, ag, da, dq, dk, dv, x, dm, normed,
        moved, abuf, bbuf, fbuf, rbuf, dgk, dgg, gpair, gmid, gfar, ogrid, a0, a1, b0, b1, qa0, qa1, qb0,
        qb1, ma0, ma1, mb0, mb1, mc0, mc1, md0, md1, lsem, ssem, rsem,
    ) = refs[25:]
    base, local = first_expert()
    r, rq = expert_block(nx, ny)
    mlp_half = (2 * r + 3 * rq) // 2
    mlp_halves, halves = split(mlp_half), split(r)
    mlp_later = [slice(mlp_half + s.start, mlp_half + s.stop) for s in mlp_halves]
    link = Link(ssem, rsem)
    load = fetch(
        [(grads_hbm.at[pl.ds(2, 2)], pbuf.at[pl.ds(2, 2)])]
        + [
            (
                wo_hbm.at[pl.ds(local, 2), :, :, :, pl.ds(512 * k, 512)],
                wo.at[:, :, :, rq * k : rq * k + rq],
            )
            for k in range(3)
        ]
        + [(a_hbm, abuf_), (q_hbm, qbuf), (k_hbm, kbuf), (v_hbm, vbuf)]
        + [(wq_hbm.at[pl.ds(local, 2)], wq), (kv_hbm, kv)]
        + [(grads_hbm.at[pl.ds(0, 2)], pbuf.at[pl.ds(0, 2)])]
        + [(n_hbm.at[0], normed), (x_hbm, x), (dm_hbm, dm)],
        lsem,
    )
    greet([flip("c"), flip("zl", "zh")] + around(("x", "y")))
    mlp_rings = [
        Ring(link, "y", lambda i, h: sa_ref.at[0, i, mlp_halves[h]], ma0, ma1),
        Ring(link, "x", lambda i, h: sb_ref.at[0, i, mlp_halves[h]], mb0, mb1),
        Ring(link, "y", lambda i, h: sa_ref.at[1, i, mlp_halves[h]], mc0, mc1),
        Ring(link, "x", lambda i, h: sb_ref.at[1, i, mlp_halves[h]], md0, md1),
    ]
    for ring in mlp_rings:
        ring.start()
    dgk[...] = jnp.zeros_like(dgk)
    dgg[...] = jnp.zeros_like(dgg)

    def spread(s):
        rows = slice(PAD * s, PAD * s + PAD)
        spread_rows = mm(places(mbuf[s], 0, base), pbuf[s]).astype(BF16)
        dr[0, rows] = spread_rows[:PAD]
        dr[1, rows] = spread_rows[PAD:]

    def outward(first):
        group = slice(PAD * first, PAD * first + 2 * PAD)
        for e in range(2):
            grad = sum(
                mm(
                    dr[e, group, 512 * k : 512 * k + 512],
                    wo[e, :, :, rq * k : rq * k + rq].reshape(FF, 512),
                    NT,
                )
                for k in range(3)
            )
            attended = abuf_[e, group].astype(F32)
            grad_gate = jnp.sum(attended * grad, axis=1, keepdims=True)
            gate = jnp.concatenate(
                [slot_gate(mbuf[first + n], gbuf[first + n], 0, base + e) for n in range(2)], axis=0
            )
            for n in range(2):
                s = first + n
                (dgg if s % 2 else dgk)[s // 2, 0:2] += token_sums(
                    mbuf[s], 0, base + e, grad_gate[PAD * n : PAD * n + PAD]
                )
            ag[e, group] = (gate * attended).astype(BF16)
            da[e, group] = (gate * grad).astype(BF16)

    masks = head_masks()
    scale = HD ** (-0.5)
    collect = Collect(
        link, pbuf.at[0], pbuf.at[1], pbuf.at[2], pbuf.at[3], abuf, bbuf, fbuf, rbuf
    )

    def scores_back(s):
        rows = slice(PAD * s, PAD * s + PAD)
        dk[...] = jnp.zeros_like(dk)
        dv[...] = jnp.zeros_like(dv)
        columns = mbuf[s].astype(F32).T
        for pair in range(4):
            cols = slice(128 * pair, 128 * pair + 128)
            kt[cols] = kbuf[s, :, cols].astype(F32).T.astype(BF16)

        def block(e, carry):
            allowed = slot_mask(columns, base + e)
            turned = []
            for pair in range(4):
                cols = slice(128 * pair, 128 * pair + 128)
                q = two_heads(qbuf[e, rows, cols], masks)
                grad = two_heads(da[e, rows, cols], masks)
                probs = softmax_keys(mm(kbuf[s, :, cols], q, NT), allowed)
                grad_probs = mm(vbuf[s, :, cols], grad, NT)
                grad_scores = []
                for h in range(2):
                    gp = grad_probs[:, PAD * h : PAD * h + PAD]
                    inner = jnp.sum(gp * probs[h], axis=0, keepdims=True)
                    grad_scores.append((probs[h] * (gp - inner)).astype(BF16))
                probs = jnp.concatenate([p.astype(BF16) for p in probs], axis=1)
                grad_scores = jnp.concatenate(grad_scores, axis=1)
                dv[:, cols] += mm(probs, grad)
                dk[:, cols] += mm(grad_scores, q)
                turned.append(own_lanes(mm(kt[cols], grad_scores)) * scale)
            depth = slot_depth(mbuf[s], base + e)
            dq[e, rows] = turn(jnp.concatenate(turned, axis=1), depth, -1.0).astype(BF16)
            return carry

        lax.fori_loop(0, 2, block, 0)
        depth = as_column(mbuf[s, 7:8].astype(F32))
        tokens = slice(TOK * s, TOK * s + TOK)
        dkv_ref[tokens, 0:QW] = turn(dk[...] * scale, depth, -1.0).astype(BF16)
        dkv_ref[tokens, QW:] = dv[...].astype(BF16)

    def rows_back(first):
        group = slice(PAD * first, PAD * first + 2 * PAD)
        for e in range(2):
            moved[e] = mm(dq[e, group], wq[e], NT).astype(BF16)
        for n in (1, 0):
            s = first + n
            both = jnp.concatenate([moved[e, PAD * n : PAD * n + PAD] for e in range(2)], axis=0)
            total = mm(places(mbuf[s], 0, base), both, TN)
            tokens = slice(TOK * s, TOK * s + TOK)
            pbuf[s] = (total + mm(dkv_ref[tokens], kv[...], NT)).astype(BF16)
            if s == 3:
                collect.send_far_mate()
            if s == 1:
                collect.send_mate()

    for copy in load[:5]:
        copy.wait()
    spread(3)
    spread(2)
    outward(2)
    for copy in load[5:10]:
        copy.wait()
    scores_back(3)
    for ring in mlp_rings:
        ring.middle()
    scores_back(2)
    rows_back(2)
    collect.forward()

    load[10].wait()
    spread(1)
    spread(0)
    outward(0)
    pairs = Pairs(link, dgk, dgg, gpair, gmid, gfar)
    o_rings = [
        Ring(link, "x", lambda i, h: ogrid.at[0, i, :, halves[h]], a0, a1),
        Ring(link, "y", lambda i, h: ogrid.at[1, :, i, halves[h]], b0, b1),
    ]
    q_rings = [
        Ring(link, "x", lambda i, h: wo.at[0, i, :, halves[h]], qa0, qa1),
        Ring(link, "y", lambda i, h: wo.at[1, :, i, halves[h]], qb0, qb1),
    ]
    wide, narrow = D // nx, FF // nx
    for e in range(2):
        for t in range(nx):
            block = mm(ag[e, :, narrow * t : narrow * t + narrow], dr[e], TN).astype(BF16)
            for k in range(3):
                ogrid[e, t, :, rq * k : rq * k + rq] = block[:, 512 * k : 512 * k + 512].reshape(
                    ny, rq, 512
                )
        o_rings[e].start()
    rows_load = pltpu.make_async_copy(r_hbm, dr, lsem.at[14])
    rows_load.start()
    pairs.forward()
    scores_back(1)
    for n, ring in enumerate(mlp_rings):
        ring.end(keeper(tm, (mlp_halves, mlp_later)[n % 2], n // 2))
    for ring in o_rings:
        ring.middle()
    scores_back(0)
    rows_back(0)

    rows_load.wait()
    for e in range(2):
        for t in range(nx):
            block = mm(dr[e, :, wide * t : wide * t + wide], dq[e], TN)
            wo[e, t] = block.astype(BF16).reshape(ny, r, QW)
        q_rings[e].start()
    o_halves = [slice(r + s.start, r + s.stop) for s in halves]
    for ring, out in zip(o_rings, (oa_ref, ob_ref)):
        ring.end(keeper(out, o_halves))

    for copy in load[11:]:
        copy.wait()
    logits = logit_grads(mbuf[0], 0, gbuf[0], pairs.total())
    router_grad_ref[...] = mm(logits, normed[...])
    gain_grad_ref[...] = jnp.zeros_like(gain_grad_ref)
    for j in range(CHUNKS):
        if j == CHUNKS - 1:
            for ring in q_rings:
                ring.middle()
        grad = collect.total(j) + mm(logits[:, part(j)], router_ref[...], TN)
        own = x[part(j)].astype(F32)
        inverse = lax.rsqrt(jnp.mean(own * own, axis=-1, keepdims=True) + EPS)
        gain_grad_ref[...] += jnp.sum(grad * (own * inverse), axis=0, keepdims=True)
        weighted = grad * gain_ref[...].reshape(1, D)
        inner = jnp.mean(weighted * own, axis=-1, keepdims=True)
        input_grad[part(j)] = (
            dm[part(j)] + inverse * weighted - own * (inverse * inverse * inverse * inner)
        ).astype(BF16)
    saved = pltpu.make_async_copy(input_grad, input_grad_hbm, lsem.at[15])
    saved.start()
    for ring, out in zip(q_rings, (oa_ref, ob_ref)):
        ring.end(keeper(out, halves))
    pairs.close()
    collect.close()
    for ring in mlp_rings + o_rings + q_rings:
        ring.close()
    saved.wait()


def attn_back_call(nx, ny, *operands):
    r, rq = expert_block(nx, ny)
    mlp_block, block = 2 * r + 3 * rq, r
    copies = 4 * CHUNKS + 2 + 8 * 6
    narrow = pltpu.VMEM((2, 4 * PAD, QW), BF16)
    grid = pltpu.VMEM((2, nx, ny, block, 512), BF16)
    return pl.pallas_call(
        partial(attn_back_kernel, nx, ny),
        out_shape=(
            jax.ShapeDtypeStruct((1, D), F32),
            jax.ShapeDtypeStruct((8, D), F32),
            jax.ShapeDtypeStruct((4 * TOK, 2 * QW), BF16),
            jax.ShapeDtypeStruct((2, mlp_block, 512), F32),
            jax.ShapeDtypeStruct((ny, r + 3 * rq, 512), BF16),
            jax.ShapeDtypeStruct((nx, r + 3 * rq, 512), BF16),
            jax.ShapeDtypeStruct((TOK, D), BF16),
        ),
        in_specs=[VSPEC] * 6 + [ANY] * 12,
        out_specs=(VSPEC,) * 6 + (ANY,),
        scratch_shapes=[
            ROWS_BUF,
            pltpu.VMEM((4, TOK, D), BF16),
            pltpu.VMEM((4, TOK, QW), BF16),
            pltpu.VMEM((4, TOK, QW), BF16),
            pltpu.VMEM((QW, TOK), BF16),
            narrow,
            narrow,
            pltpu.VMEM((2, D, QW), BF16),
            grid,
            pltpu.VMEM((D, 2 * QW), BF16),
            pltpu.VMEM((2, 4 * PAD, D), BF16),
            narrow,
            narrow,
            narrow,
            pltpu.VMEM((TOK, QW), F32),
            pltpu.VMEM((TOK, QW), F32),
            ROWS_BUF,
            pltpu.VMEM((TOK, D), F32),
            ROWS_BUF,
            pltpu.VMEM((2, 2 * PAD, D), BF16),
        ]
        + [ROWS_BUF] * 4
        + [
            pltpu.VMEM((2, 8, TOK), F32),
            pltpu.VMEM((2, 8, TOK), F32),
            pltpu.VMEM((2, 8, TOK), F32),
            pltpu.VMEM((8, TOK), F32),
            pltpu.VMEM((8, TOK), F32),
            grid,
        ]
        + (ring_buffers((ny,), block) + ring_buffers((nx,), block)) * 2
        + ring_buffers((), mlp_block // 2) * 4
        + [
            pltpu.SemaphoreType.DMA((16,)),
            pltpu.SemaphoreType.DMA((copies,)),
            pltpu.SemaphoreType.DMA((copies,)),
        ],
        compiler_params=remote_params(63, 3),
        cost_estimate=pl.CostEstimate(flops=10**9, bytes_accessed=300 * 10**6, transcendentals=0),
        name="attention_backward",
    )(*operands)


def last_kernel(nx, ny, *refs):
    (
        small_a, small_b, small_c, small_d, middle_ref, tm, sa_ref, sb_ref, keep_hbm, give_hbm, n_hbm,
        dkv_hbm,
    ) = refs[:12]
    outs = refs[12:22]
    (
        output_ref, kv_ref, first_ref, second_ref, norm_ref, gate_ref, up_ref, down_ref, query_ref, out_ref,
        nb, dkv, ga, gb, kf, ko, la, lb, fb, lr, kgrid, kgive, kback, sgrid,
        ka0, ka1, kb0, kb1, s0, s1, tka, tkb, ts,
        aa0, aa1, ab0, ab1, kka0, kka1, kkb0, kkb1, ss0, ss1, tt, tk, tsm,
        zsend, zrecv, ksend, krecv, msend, mrecv, y, csend, crecv, kcsend, kcrecv, mcsend, mcrecv,
        wsend, wrecv, lsem, osem, ssem, rsem,
    ) = refs[22:]
    zl, core, zh = lax.axis_index("zl"), lax.axis_index("c"), lax.axis_index("zh")
    r, rq = expert_block(nx, ny)
    halves, k_halves, s_halves = split(r + 3 * rq), split(r // 2), split(r)
    link = Link(ssem, rsem)
    load = fetch(
        [(give_hbm.at[1], ga), (give_hbm.at[0], gb), (n_hbm, nb), (dkv_hbm, dkv)]
        + [(keep_hbm.at[1], kf), (keep_hbm.at[0], ko)],
        lsem,
    )
    saved = []

    def save(*numbers):
        for n in numbers:
            copy = pltpu.make_async_copy(refs[22 + n], outs[n], osem.at[n])
            copy.start()
            saved.append(copy)

    mate, far = flip("c"), flip("zl", "zh")
    greet([mate, far, flip("zl"), flip("zh")] + around(("x", "y")))
    seconds = [
        Ring(link, "y", lambda i, h: sa_ref.at[i, halves[h]], aa0, aa1),
        Ring(link, "x", lambda i, h: sb_ref.at[i, halves[h]], ab0, ab1),
    ]
    k_rings = [
        Ring(link, "x", lambda i, h: kgrid.at[0, i, :, k_halves[h]], ka0, ka1),
        Ring(link, "y", lambda i, h: kgrid.at[1, :, i, k_halves[h]], kb0, kb1),
    ]
    s_ring = Ring(link, "x", lambda i, h: sgrid.at[i, :, s_halves[h]], s0, s1)
    for ring in seconds:
        ring.start()
    load[0].wait()
    load[1].wait()
    late_first = link.copy(ga, la, mate)
    late_second = link.copy(gb, lb, mate)
    row = iota((8, 1), 0)
    norms = jnp.where(row == 0, small_c[...], jnp.where(row == 1, small_d[...], 0.0))
    small = jnp.concatenate(
        [small_a[...], small_b[...], norms, jnp.zeros((104, D), F32)], axis=0
    ).T
    sgrid[...] = small.astype(BF16).reshape(nx, ny, r, 128)
    s_ring.start()
    for copy in load[2:5]:
        copy.wait()
    late_first.wait_recv()
    fb[...] = (kf[...].astype(F32) + la[...].astype(F32)).astype(BF16)
    late_third = link.copy(fb, lr, far)

    wide = D // nx

    def project(side, target):
        columns = pl.ds(pl.multiple_of(side * QW, QW), QW)
        for t in range(nx):
            block = sum(
                mm(nb[s, :, wide * t : wide * t + wide], dkv[TOK * s : TOK * s + TOK, columns], TN)
                for s in range(4)
            )
            block = block.astype(BF16).reshape(ny, 2, r // 2, QW)
            for h in range(2):
                target[h, t] = block[:, h]

    project(1 - core, kgive)
    k_copy = link.copy(kgive, kback, mate)
    for ring in seconds:
        ring.middle()
    s_ring.middle()
    project(core, kgrid)
    k_copy.wait_recv()
    kgrid[...] = (kgrid[...].astype(F32) + kback[...].astype(F32)).astype(BF16)
    for ring in k_rings:
        ring.start()
    for e in range(2):
        seconds[e].end(keeper(tt, halves, e))

    fields = [(tm, 0, r), (tm, r, r)] + [(tm, 2 * r + rq * k, rq) for k in range(3)]
    fields += [(tt, 0, r)] + [(tt, r + rq * k, rq) for k in range(3)]
    to_zl = flip("zl")
    halves_to_send(fields, zsend, zl)
    z_copy = link.copy(zsend, zrecv, to_zl)
    s_ring.end(keeper(ts, s_halves))
    s_second = Ring(link, "y", lambda i, h: ts.at[i, s_halves[h]], ss0, ss1)
    s_second.start()
    for ring in k_rings:
        ring.middle()
    z_copy.wait_recv()
    add_halves(fields, zrecv, y, zl)
    quarters_to_send(fields, y, csend, core)
    c_copy = link.copy(csend, crecv, mate)
    s_second.middle()
    k_seconds = [
        Ring(link, "y", lambda i, h: tka.at[i, k_halves[h]], kka0, kka1),
        Ring(link, "x", lambda i, h: tkb.at[i, k_halves[h]], kkb0, kkb1),
    ]
    for e in range(2):
        k_rings[e].end(keeper((tka, tkb)[e], k_halves))
        k_seconds[e].start()
    c_copy.wait_recv()
    targets = [(gate_ref, None), (up_ref, None)] + [(down_ref, k) for k in range(3)]
    targets += [(query_ref, None)] + [(out_ref, k) for k in range(3)]
    place_quarters(fields, targets, y, crecv, core)
    save(5, 6, 7, 8, 9)
    for ring in k_seconds:
        ring.middle()

    def store_small(h, value):
        tsm[s_halves[h]] = value

    s_second.end(store_small)
    for e in range(2):
        k_seconds[e].end(keeper(tk, k_halves, e))
    ksend[...] = tk[1 - zl].astype(BF16)
    msend[...] = tsm[pl.ds(pl.multiple_of((1 - zl) * (r // 2), 8), r // 2)].astype(BF16)
    k_copies = [link.copy(a, b, to_zl) for a, b in ((ksend, krecv), (msend, mrecv))]
    for copy in k_copies:
        copy.wait_recv()
    k_own = tk[zl] + krecv[...].astype(F32)
    m_own = tsm[pl.ds(pl.multiple_of(zl * (r // 2), 8), r // 2)] + mrecv[...].astype(F32)
    tk[0] = k_own
    tsm[0 : r // 2] = m_own

    quarter = r // 4
    kcsend[...] = tk[0, pl.ds(pl.multiple_of((1 - core) * quarter, 8), quarter)]
    mcsend[...] = tsm[pl.ds(pl.multiple_of((1 - core) * quarter, 8), quarter)]
    m_copies = [link.copy(a, b, mate) for a, b in ((kcsend, kcrecv), (mcsend, mcrecv))]
    for copy in m_copies:
        copy.wait_recv()
    k_own = tk[0, pl.ds(pl.multiple_of(core * quarter, 8), quarter)]
    k_other = kcrecv[...]
    first = core == 0
    wsend[:, 0:QW] = jnp.where(first, k_own, k_other)
    wsend[:, QW : 2 * QW] = jnp.where(first, k_other, k_own)
    wsend[:, 2 * QW :] = tsm[pl.ds(pl.multiple_of(core * quarter, 8), quarter)] + mcrecv[...]
    w_copy = link.copy(wsend, wrecv, flip("zh"))
    load[5].wait()
    late_second.wait_recv()
    late_third.wait_recv()
    for j in range(CHUNKS):
        output_ref[part(j)] = (
            middle_ref[part(j)]
            + ko[part(j)].astype(F32)
            + lb[part(j)].astype(F32)
            + lr[part(j)].astype(F32)
        ).astype(BF16)
    save(0)
    w_copy.wait_recv()
    total = wsend[...] + wrecv[...]
    total = jnp.where(zh == 0, total[0 : r // 8], total[r // 8 :])
    kv_ref[...] = total[:, 0 : 2 * QW]
    first_ref[...] = total[:, 2 * QW : 2 * QW + 8]
    second_ref[...] = total[:, 2 * QW + 8 : 2 * QW + 16]
    norm_ref[...] = total[:, 2 * QW : 2 * QW + 128].T[16:24]
    save(1, 2, 3, 4)
    for ring in seconds + k_rings + [s_ring] + k_seconds + [s_second]:
        ring.close()
    for copy in [late_first, late_second, late_third, k_copy, z_copy, c_copy, w_copy] + k_copies + m_copies:
        copy.wait_send()
    for copy in saved:
        copy.wait()


def last_call(nx, ny, *operands):
    r, rq = expert_block(nx, ny)
    block, mlp_block, k_block = r + 3 * rq, 2 * r + 3 * rq, r // 2
    zrows = (block + mlp_block) // 2

    def small_buffers(lead):
        return [pltpu.VMEM((3,) + lead + (s.stop - s.start, 128), BF16) for s in split(r)]

    copies = 4 * 12 + 11
    results = [
        ((TOK, D), BF16),
        ((r // 8, 2 * QW), F32),
        ((r // 8, 8), F32),
        ((r // 8, 8), F32),
        ((8, r // 8), F32),
        ((4, r // 4, FF), F32),
        ((4, r // 4, FF), F32),
        ((4, rq // 4, D), F32),
        ((4, r // 4, QW), F32),
        ((4, rq // 4, D), F32),
    ]
    return pl.pallas_call(
        partial(last_kernel, nx, ny),
        out_shape=tuple(jax.ShapeDtypeStruct(*a) for a in results),
        in_specs=[VSPEC] * 8 + [ANY] * 4,
        out_specs=(ANY,) * len(results),
        scratch_shapes=[pltpu.VMEM(*a) for a in results]
        + [
            pltpu.VMEM((4, TOK, D), BF16),
            pltpu.VMEM((4 * TOK, 2 * QW), BF16),
        ]
        + [ROWS_BUF] * 8
        + [
            pltpu.VMEM((2, nx, ny, k_block, 512), BF16),
            pltpu.VMEM((2, nx, ny, k_block, 512), BF16),
            pltpu.VMEM((2, nx, ny, k_block, 512), BF16),
            pltpu.VMEM((nx, ny, r, 128), BF16),
        ]
        + ring_buffers((ny,), k_block)
        + ring_buffers((nx,), k_block)
        + small_buffers((ny,))
        + [
            pltpu.VMEM((ny, k_block, 512), BF16),
            pltpu.VMEM((nx, k_block, 512), BF16),
            pltpu.VMEM((ny, r, 128), BF16),
        ]
        + ring_buffers((), block) * 2
        + ring_buffers((), k_block) * 2
        + small_buffers(())
        + [
            pltpu.VMEM((2, block, 512), F32),
            pltpu.VMEM((2, k_block, 512), F32),
            pltpu.VMEM((r, 128), F32),
            pltpu.VMEM((2, zrows, 512), BF16),
            pltpu.VMEM((2, zrows, 512), BF16),
            pltpu.VMEM((k_block, 512), BF16),
            pltpu.VMEM((k_block, 512), BF16),
            pltpu.VMEM((r // 2, 128), BF16),
            pltpu.VMEM((r // 2, 128), BF16),
            pltpu.VMEM((2, zrows, 512), F32),
            pltpu.VMEM((2, zrows // 2, 512), F32),
            pltpu.VMEM((2, zrows // 2, 512), F32),
            pltpu.VMEM((r // 4, 512), F32),
            pltpu.VMEM((r // 4, 512), F32),
            pltpu.VMEM((r // 4, 128), F32),
            pltpu.VMEM((r // 4, 128), F32),
            pltpu.VMEM((r // 4, 2 * QW + 128), F32),
            pltpu.VMEM((r // 4, 2 * QW + 128), F32),
            pltpu.SemaphoreType.DMA((6,)),
            pltpu.SemaphoreType.DMA((len(results),)),
            pltpu.SemaphoreType.DMA((copies,)),
            pltpu.SemaphoreType.DMA((copies,)),
        ],
        compiler_params=remote_params(60, 4),
        cost_estimate=pl.CostEstimate(flops=10**9, bytes_accessed=150 * 10**6, transcendentals=0),
        name="last_sums",
    )(*operands)


def copy_kernel(norms_ref, *refs):
    n = (len(refs) - 4) // 3
    sources, targets, (first, second), bufs = refs[:n], refs[n : 2 * n], refs[2 * n : 2 * n + 2], refs[2 * n + 2 : -2]
    came = fetch(list(zip(sources, bufs)), refs[-2])
    first[...] = norms_ref[1]
    second[...] = norms_ref[0]
    left = []
    for k in range(n):
        came[k].wait()
        copy = pltpu.make_async_copy(bufs[k], targets[k], refs[-1].at[k])
        copy.start()
        left.append(copy)
    for copy in left:
        copy.wait()


def copy_call(norms, *arrays):
    count, n = norms.shape[1], len(arrays)
    return pl.pallas_call(
        copy_kernel,
        out_shape=tuple(jax.ShapeDtypeStruct(a.shape, a.dtype) for a in arrays)
        + (jax.ShapeDtypeStruct((count,), F32),) * 2,
        in_specs=[VSPEC] + [ANY] * n,
        out_specs=(ANY,) * n + (VSPEC,) * 2,
        scratch_shapes=[pltpu.VMEM(a.shape, a.dtype) for a in arrays]
        + [pltpu.SemaphoreType.DMA((n,)), pltpu.SemaphoreType.DMA((n,))],
        compiler_params=params(60),
        name="results",
    )(norms, *arrays)


def per_device(
    inputs, cotangent, norm_one, kv_weight, attn_router, query_experts, out_experts, norm_two,
    mlp_router, gate_experts, up_experts, down_experts, attn_routes, mlp_routes, slot_order,
    seg_lengths, seg_parents,
):
    nx, ny = lax.axis_size("x"), lax.axis_size("y")
    router_one, router_two = attn_router.T, mlp_router.T
    normed, keys, values, rows, q, attended, normed_twos, cots, gates, metas, middle = forward_call(
        seg_lengths, seg_parents, slot_order, jnp.swapaxes(attn_routes, 2, 3),
        jnp.swapaxes(mlp_routes, 2, 3), inputs, norm_one, norm_two,
        router_one, cotangent, kv_weight, query_experts, out_experts,
    )
    r, rq = expert_block(nx, ny)
    grad_middle, grad_norm_two, grad_router_two, sums_a, sums_b, grads_in, keep_out, give_out = mlp_call(
        nx, ny, metas, router_two, norm_two, normed_twos, cotangent, cots, middle,
        gate_experts.reshape(4, nx, ny, r, FF), up_experts.reshape(4, nx, ny, r, FF),
        down_experts.reshape(4, nx, ny, rq, D),
    )
    grad_norm_one, grad_router_one, grad_kv, sums_mlp, sums_a, sums_b, input_grad = attn_back_call(
        nx, ny, metas, gates, router_one, norm_one, sums_a, sums_b, inputs, grad_middle, normed,
        grads_in, keys, values, q, attended, query_experts, out_experts.reshape(4, nx, ny, rq, D),
        kv_weight, rows,
    )
    output, kv, router_one_grad, router_two_grad, norms, gate, up, down, query, out = last_call(
        nx, ny, grad_router_one, grad_router_two, grad_norm_two, grad_norm_one, middle, sums_mlp, sums_a,
        sums_b, keep_out, give_out, normed, grad_kv,
    )
    (
        output, input_grad, kv, router_one_grad, query, out, router_two_grad, gate, up, down, norm_one_grad,
        norm_two_grad,
    ) = copy_call(
        norms, output, input_grad, kv, router_one_grad, query, out, router_two_grad, gate, up, down
    )
    return (
        output, input_grad, norm_one_grad, kv, router_one_grad, query, out, norm_two_grad,
        router_two_grad, gate, up, down,
    )


def solution(mesh):
    total = mesh.devices.size
    grid = mesh.devices.reshape(4, total // 32, 2, 2, 2)
    fine = Mesh(grid, ("x", "y", "zl", "c", "zh"))
    copies = ("x", "y", "zl", "c")
    every = copies + ("zh",)
    weight = P("zh", None, None)
    placed = (
        P(every, None),
        P(every, None),
        P(),
        P(),
        P(),
        weight,
        weight,
        P(),
        P(),
        weight,
        weight,
        weight,
        P(copies, None, None, None),
        P(copies, None, None, None),
        P(copies, None, None, None),
        P(copies, None, None),
        P(copies, None, None),
    )
    grad = P("zh", copies, None)
    return jax.shard_map(
        per_device,
        mesh=fine,
        in_specs=placed,
        out_specs=(
            P(every, None),
            P(every, None),
            P(every),
            P(every, None),
            P(every, None),
            grad,
            grad,
            P(every),
            P(every, None),
            grad,
            grad,
            grad,
        ),
        check_vma=False,
    )
```

time: 2330 us -> 337 us (0.14)
  waiting for transfers between devices: 1030 us -> 0 us
  blocking collectives: 518 us -> 0 us
  local copies, waits for them, and re-layouts: 338 us -> 2.72 us
  Pallas kernels: 0 us -> 327 us
  matrix products: 147 us -> 0 us
  other arithmetic: 136 us -> 0 us
  starting transfers between devices: 128 us -> 0 us
    reduce_scatter x5 -> x0, waiting for transfers between devices: 916 us -> none  [the longest x1 307 us: per_device(): lax.psum_scatter(grad_out, 'dp', scatter_dimension=1, tiled=True)]
    unnamed x1 -> x0, blocking collectives: 424 us -> none
    pallas_call x0 -> x5, Pallas kernels: none -> 327 us  [the longest x1 131 us: forward_call(): pl.pallas_call(forward_kernel, out_shape=(rows, heads, heads, jax.ShapeDt...]
    dot_general x31 -> x0, matrix products: 147 us -> none  [the longest x1 8.79 us: per_device(): jnp.einsum('slcd,slcq->ldq', attn_recv, grad_query_pre, preferred_element...]
    all_to_all x6 -> x0, waiting for transfers between devices: 114 us -> none  [the longest x1 28.7 us: per_device(): lax.all_to_all(attn_grad_send, 'expert', split_axis=0, concat_axis=0, til...]
    gather x15 -> x0, local copies, waits for them, and re-layouts: 109 us -> none  [the longest x8 69.3 us: gather_rows(): return jnp.take(padded, row_index, axis=0)]
    unnamed x35 -> x0, starting transfers between devices: 94.6 us -> none
    unnamed x227 -> x2, local copies, waits for them, and re-layouts: 91.6 us -> 2.72 us
  transfers between devices with their start and end apart: 46 -> 0, of which waited for: 9 -> 0; matrix products, arithmetic and copies ran while one was open for 30% -> 0% of each run, Pallas kernels for 0% -> 0%
where the time goes in v1:
time: 337 us; the launch traced here: 330 us
  Pallas kernels  327 us (97%)
    pallas_call x1, Pallas kernels, forward_call(): pl.pallas_call(forward_kernel, out_shape=(rows, heads, heads, jax.ShapeDt...  131 us
    pallas_call x1, Pallas kernels, mlp_call(): pl.pallas_call(partial(mlp_kernel, nx, ny), out_shape=(jax.ShapeDtypeStru...  75.2 us
    pallas_call x1, Pallas kernels, attn_back_call(): pl.pallas_call(partial(attn_back_kernel, nx, ny), out_shape=(jax.ShapeDty...  68.5 us
    pallas_call x1, Pallas kernels, last_call(): pl.pallas_call(partial(last_kernel, nx, ny), out_shape=tuple((jax.ShapeDt...  47.6 us

profile of v1, /device:TPU:1, one launch (start us, length us, event | category | flops | bytes accessed | tf_op | source)
XLA Modules:
  0.0 330.5 jit_solution(16479221785013200989)
XLA Ops:
  0.6 131.0 %attention_forward.1 = (bf16[4,384,1536]{2,1,0:T(8,128)(2,1)}, bf16[4,384,512]{2,1,0:T(8,128)(2,1)}, bf16[4,384,512]{2,1,0:T(8,128)(2,1)}, bf16[2,512,1536]{2,1,...) custom-call(s32[1,2,13]{2,1,0:T(2,128)} %refs_0_.1, ...), custom_call_target="tpu_custom_call" | custom-call | flops 1000000000 | bytes 300000000 | tf_op jit(solution)/shard_map/attention_forward/pallas_call | solution.py:639
  131.7 75.2 %feed_forward.1 = (f32[384,1536]{1,0:T(8,128)}, f32[1,1536]{1,0:T(1,128)}, f32[8,1536]{1,0:T(8,128)}, bf16[2,4,144,512]{3,2,1,0:T(8,128)(2,1)}, bf16[2,4,144,512...) custom-call(s32[4,8,384]{2,1,0:T(8,128)} %get-tuple-element.60.refs_, ...), custom_call_target="tpu_custom_call" | custom-call | flops 1000000000 | bytes 250000000 | tf_op jit(solution)/shard_map/feed_forward/pallas_call | solution.py:894
  206.8 68.5 %attention_backward.1 = (f32[1,1536]{1,0:T(1,128)}, f32[8,1536]{1,0:T(8,128)}, bf16[1536,1024]{1,0:T(8,128)(2,1)}, f32[2,288,512]{2,1,0:T(8,128)}, bf16[4,192,51...) custom-call(s32[4,8,384]{2,1,0:T(8,128)} %get-tuple-element.60.refs_0_, ...), custom_call_target="tpu_custom_call" | custom-call | flops 1000000000 | bytes 300000000 | tf_op jit(solution)/shard_map/attention_backward/pallas_call | solution.py:1219
  275.4 47.6 %last_sums.1 = (bf16[384,1536]{1,0:T(8,128)(2,1)}, f32[12,1024]{1,0:T(8,128)}, f32[12,8]{1,0:T(8,128)}, f32[12,8]{1,0:T(8,128)}, f32[8,12]{1,0:T(8,128)}, /*inde...) custom-call(f32[8,1536]{1,0:T(8,128)} %get-tuple-element.75.refs_0_,, ...), custom_call_target="tpu_custom_call" | custom-call | flops 1000000000 | bytes 150000000 | tf_op jit(solution)/shard_map/last_sums/pallas_call | solution.py:1470
  322.9 4.4 %results.1 = (bf16[384,1536]{1,0:T(8,128)(2,1)}, bf16[384,1536]{1,0:T(8,128)(2,1)}, f32[12,1024]{1,0:T(8,128)}, f32[12,8]{1,0:T(8,128)}, f32[4,24,512]{2,1,0:T(8...) custom-call(f32[8,12]{1,0:T(8,128)} %get-tuple-element.85.norms_ref,, ...), custom_call_target="tpu_custom_call" | custom-call | tf_op jit(solution)/shard_map/results/pallas_call | solution.py:1546
  327.3 1.4 copy.29
  328.7 1.4 copy.30

commit v2 on v1

--- a/solution.py
+++ b/solution.py
@@ -214,13 +214,8 @@
     return jnp.concatenate([rows * masks[0], rows * masks[1]], axis=0)
 
 
-def softmax_keys(scores, allowed):
-    probs = []
-    for h in range(2):
-        one = jnp.where(allowed, scores[:, PAD * h : PAD * h + PAD] * HD ** (-0.5), -1e30)
-        raised = jnp.exp(one - jnp.max(one, axis=0, keepdims=True))
-        probs.append(raised * (1.0 / jnp.sum(raised, axis=0, keepdims=True)))
-    return probs
+def masked(scores, allowed, h):
+    return jnp.where(allowed, scores[:, PAD * h : PAD * h + PAD], -1e30)
 
 
 def own_lanes(both):
@@ -239,9 +234,9 @@
     return total.astype(BF16)
 
 
-def head_masks():
+def head_masks(weight=1.0):
     lane = iota((1, 128), 1)
-    return (lane < 64).astype(F32).astype(BF16), (lane >= 64).astype(F32).astype(BF16)
+    return [jnp.where(half, weight, 0.0).astype(BF16) for half in (lane < 64, lane >= 64)]
 
 
 def fetch(pairs, sems):
@@ -493,7 +488,7 @@
     (
         len_ref, par_ref, order_ref, routes_one, routes_two, x_ref, gain_ref, gain_two_ref, router_ref,
         cot_ref, kv_hbm, wq_hbm, wo_hbm,
-        n_hbm, k_hbm, v_hbm, r_hbm, q_hbm, a_hbm, n2_hbm, cots_hbm, gate_ref, meta_ref, middle_ref,
+        n_hbm, k_hbm, v_hbm, r_hbm, q_hbm, a_hbm, n2_hbm, cots_hbm, gate_ref, meta_ref, middle_ref, lse_ref,
         xb, nb, kb, vb, vt, columns, rb, qb, ab, obuf, pb, kv, wq, wo, mbuf, abuf, bbuf, fbuf, rbuf, own,
         landed, cb, wsem, osem, sems, ssem, rsem,
     ) = refs
@@ -544,7 +539,7 @@
             save(rb.at[e, pl.ds(PAD * s, PAD)], r_hbm.at[e, pl.ds(PAD * s, PAD)])
         gate_ref[s, 0:2] = pair_gates(meta, 0, mm(router_ref[...], normed, NT))
 
-    masks = head_masks()
+    masks = head_masks(HD ** (-0.5))
 
     def attend(first, between=None):
         group = slice(PAD * first, PAD * first + 2 * PAD)
@@ -561,8 +556,16 @@
             for pair in range(4):
                 cols = slice(128 * pair, 128 * pair + 128)
                 q = two_heads(qb[e, pl.ds(start, PAD), cols], masks)
-                probs = softmax_keys(mm(kb[s, :, cols], q, NT), allowed)
-                probs = jnp.concatenate([p.astype(BF16) for p in probs], axis=1)
+                scores = mm(kb[s, :, cols], q, NT)
+                probs = []
+                for h in range(2):
+                    one = masked(scores, allowed, h)
+                    top = jnp.max(one, axis=0, keepdims=True)
+                    raised = jnp.exp(one - top)
+                    total = jnp.sum(raised, axis=0, keepdims=True)
+                    lse_ref[e, s, 2 * pair + h : 2 * pair + h + 1] = top + jnp.log(total)
+                    probs.append((raised * (1.0 / total)).astype(BF16))
+                probs = jnp.concatenate(probs, axis=1)
                 ab[e, pl.ds(start, PAD), cols] = own_lanes(mm(vt[s, cols], probs)).astype(BF16)
             return carry
 
@@ -650,9 +653,10 @@
             jax.ShapeDtypeStruct((4, 8, TOK), F32),
             jax.ShapeDtypeStruct((4, 8, TOK), I32),
             jax.ShapeDtypeStruct((TOK, D), F32),
+            jax.ShapeDtypeStruct((2, 4, KVH, PAD), F32),
         ),
         in_specs=[SSPEC] * 2 + [VSPEC] * 8 + [ANY] * 3,
-        out_specs=(ANY,) * 8 + (VSPEC,) * 3,
+        out_specs=(ANY,) * 8 + (VSPEC,) * 4,
         scratch_shapes=[
             pltpu.VMEM((3, TOK, D), BF16),
             pltpu.VMEM((4, TOK, D), BF16),
@@ -692,11 +696,11 @@
 def mlp_kernel(nx, ny, *refs):
     (
         mbuf, router_ref, gain_ref, n4_hbm, cot_hbm, cots_hbm, middle_hbm, wg_hbm, wu_hbm, wd_hbm,
-        dm_ref, gain_grad_ref, router_grad_ref, sa_ref, sb_ref, dm4_ref, keep_out, give_out,
+        gain_grad_ref, router_grad_ref, sa_ref, sb_ref, dm4_ref, keep_out, give_out, dm_hbm,
     ) = refs[:18]
     (
         pbuf, gb, mr, gr, dgu, hg, obuf, dbuf, big, middle, cot, normed, own, landed, abuf, bbuf, fbuf, rbuf,
-        gates, dgk, dgg, gpair, gmid, gfar, a0, a1, b0, b1, c0, c1, d0, d1, sems, lsem, osem, ssem, rsem,
+        gates, dgk, dgg, gpair, gmid, gfar, dm_ref, a0, a1, b0, b1, c0, c1, d0, d1, sems, lsem, osem, ssem, rsem,
     ) = refs[18:]
     base, local = first_expert()
     r, rq = expert_block(nx, ny)
@@ -873,6 +877,7 @@
         own[part(j)] = result.astype(BF16)
         spread.send(j)
         dm_ref[part(j)] = result
+        save(dm_ref.at[part(j)], dm_hbm.at[part(j)])
     for j in range(CHUNKS):
         spread.relay(j)
     for e in range(2):
@@ -894,7 +899,6 @@
     return pl.pallas_call(
         partial(mlp_kernel, nx, ny),
         out_shape=(
-            jax.ShapeDtypeStruct((TOK, D), F32),
             jax.ShapeDtypeStruct((1, D), F32),
             jax.ShapeDtypeStruct((8, D), F32),
             jax.ShapeDtypeStruct((2, ny, block // 2, 512), BF16),
@@ -902,9 +906,10 @@
             jax.ShapeDtypeStruct((4, TOK, D), BF16),
             part_shape,
             part_shape,
+            jax.ShapeDtypeStruct((TOK, D), F32),
         ),
         in_specs=[VSPEC] * 3 + [ANY] * 7,
-        out_specs=(VSPEC,) * 5 + (ANY,) * 3,
+        out_specs=(VSPEC,) * 4 + (ANY,) * 4,
         scratch_shapes=[
             pltpu.VMEM((4, TOK, D), BF16),
             pltpu.VMEM((4, TOK, D), BF16),
@@ -925,12 +930,13 @@
             pltpu.VMEM((2, 8, TOK), F32),
             pltpu.VMEM((8, TOK), F32),
             pltpu.VMEM((8, TOK), F32),
+            pltpu.VMEM((TOK, D), F32),
         ]
         + (ring_buffers((ny,), block // 2) + ring_buffers((nx,), block // 2)) * 2
         + [
             pltpu.SemaphoreType.DMA((2 * CHUNKS,)),
             pltpu.SemaphoreType.DMA((13,)),
-            pltpu.SemaphoreType.DMA((4,)),
+            pltpu.SemaphoreType.DMA((4 + CHUNKS,)),
             pltpu.SemaphoreType.DMA((copies,)),
             pltpu.SemaphoreType.DMA((copies,)),
         ],
@@ -993,15 +999,15 @@
 
 def attn_back_kernel(nx, ny, *refs):
     (
-        mbuf, gbuf, router_ref, gain_ref, sa_ref, sb_ref, x_hbm, dm_hbm, n_hbm, grads_hbm,
+        mbuf, gbuf, lse_ref, router_ref, gain_ref, sa_ref, sb_ref, x_hbm, dm_hbm, n_hbm, grads_hbm,
         k_hbm, v_hbm, q_hbm, a_hbm, wq_hbm, wo_hbm, kv_hbm, r_hbm,
-    ) = refs[:18]
-    gain_grad_ref, router_grad_ref, dkv_ref, tm, oa_ref, ob_ref, input_grad_hbm = refs[18:25]
+    ) = refs[:19]
+    gain_grad_ref, router_grad_ref, oa_ref, ob_ref, dkv_hbm, tm_hbm, input_grad_hbm = refs[19:26]
     (
-        input_grad, pbuf, kbuf, vbuf, kt, qbuf, abuf_, wq, wo, kv, dr, ag, da, dq, dk, dv, x, dm, normed,
+        dkv_ref, tm, input_grad, pbuf, kbuf, vbuf, kt, qbuf, abuf_, wq, wo, kv, dr, ag, da, dq, dk, dv, x, dm, normed,
         moved, abuf, bbuf, fbuf, rbuf, dgk, dgg, gpair, gmid, gfar, ogrid, a0, a1, b0, b1, qa0, qa1, qb0,
         qb1, ma0, ma1, mb0, mb1, mc0, mc1, md0, md1, lsem, ssem, rsem,
-    ) = refs[25:]
+    ) = refs[26:]
     base, local = first_expert()
     r, rq = expert_block(nx, ny)
     mlp_half = (2 * r + 3 * rq) // 2
@@ -1065,8 +1071,8 @@
             ag[e, group] = (gate * attended).astype(BF16)
             da[e, group] = (gate * grad).astype(BF16)
 
-    masks = head_masks()
     scale = HD ** (-0.5)
+    masks, q_masks = head_masks(), head_masks(scale)
     collect = Collect(
         link, pbuf.at[0], pbuf.at[1], pbuf.at[2], pbuf.at[3], abuf, bbuf, fbuf, rbuf
     )
@@ -1085,9 +1091,13 @@
             turned = []
             for pair in range(4):
                 cols = slice(128 * pair, 128 * pair + 128)
-                q = two_heads(qbuf[e, rows, cols], masks)
+                q = two_heads(qbuf[e, rows, cols], q_masks)
                 grad = two_heads(da[e, rows, cols], masks)
-                probs = softmax_keys(mm(kbuf[s, :, cols], q, NT), allowed)
+                scores = mm(kbuf[s, :, cols], q, NT)
+                probs = [
+                    jnp.exp(masked(scores, allowed, h) - lse_ref[e, s, 2 * pair + h : 2 * pair + h + 1])
+                    for h in range(2)
+                ]
                 grad_probs = mm(vbuf[s, :, cols], grad, NT)
                 grad_scores = []
                 for h in range(2):
@@ -1106,7 +1116,7 @@
         lax.fori_loop(0, 2, block, 0)
         depth = as_column(mbuf[s, 7:8].astype(F32))
         tokens = slice(TOK * s, TOK * s + TOK)
-        dkv_ref[tokens, 0:QW] = turn(dk[...] * scale, depth, -1.0).astype(BF16)
+        dkv_ref[tokens, 0:QW] = turn(dk[...], depth, -1.0).astype(BF16)
         dkv_ref[tokens, QW:] = dv[...].astype(BF16)
 
     def rows_back(first):
@@ -1160,15 +1170,24 @@
                     ny, rq, 512
                 )
         o_rings[e].start()
+    saved = []
+
+    def save(source, target):
+        copy = pltpu.make_async_copy(source, target, lsem.at[15 + len(saved)])
+        copy.start()
+        saved.append(copy)
+
     rows_load = pltpu.make_async_copy(r_hbm, dr, lsem.at[14])
     rows_load.start()
     pairs.forward()
     scores_back(1)
     for n, ring in enumerate(mlp_rings):
         ring.end(keeper(tm, (mlp_halves, mlp_later)[n % 2], n // 2))
+    save(tm, tm_hbm)
     for ring in o_rings:
         ring.middle()
     scores_back(0)
+    save(dkv_ref, dkv_hbm)
     rows_back(0)
 
     rows_load.wait()
@@ -1199,15 +1218,15 @@
         input_grad[part(j)] = (
             dm[part(j)] + inverse * weighted - own * (inverse * inverse * inverse * inner)
         ).astype(BF16)
-    saved = pltpu.make_async_copy(input_grad, input_grad_hbm, lsem.at[15])
-    saved.start()
+    save(input_grad, input_grad_hbm)
     for ring, out in zip(q_rings, (oa_ref, ob_ref)):
         ring.end(keeper(out, halves))
     pairs.close()
     collect.close()
     for ring in mlp_rings + o_rings + q_rings:
         ring.close()
-    saved.wait()
+    for copy in saved:
+        copy.wait()
 
 
 def attn_back_call(nx, ny, *operands):
@@ -1221,15 +1240,17 @@
         out_shape=(
             jax.ShapeDtypeStruct((1, D), F32),
             jax.ShapeDtypeStruct((8, D), F32),
+            jax.ShapeDtypeStruct((ny, r + 3 * rq, 512), BF16),
+            jax.ShapeDtypeStruct((nx, r + 3 * rq, 512), BF16),
             jax.ShapeDtypeStruct((4 * TOK, 2 * QW), BF16),
             jax.ShapeDtypeStruct((2, mlp_block, 512), F32),
-            jax.ShapeDtypeStruct((ny, r + 3 * rq, 512), BF16),
-            jax.ShapeDtypeStruct((nx, r + 3 * rq, 512), BF16),
             jax.ShapeDtypeStruct((TOK, D), BF16),
         ),
-        in_specs=[VSPEC] * 6 + [ANY] * 12,
-        out_specs=(VSPEC,) * 6 + (ANY,),
+        in_specs=[VSPEC] * 7 + [ANY] * 12,
+        out_specs=(VSPEC,) * 4 + (ANY,) * 3,
         scratch_shapes=[
+            pltpu.VMEM((4 * TOK, 2 * QW), BF16),
+            pltpu.VMEM((2, mlp_block, 512), F32),
             ROWS_BUF,
             pltpu.VMEM((4, TOK, D), BF16),
             pltpu.VMEM((4, TOK, QW), BF16),
@@ -1263,7 +1284,7 @@
         + (ring_buffers((ny,), block) + ring_buffers((nx,), block)) * 2
         + ring_buffers((), mlp_block // 2) * 4
         + [
-            pltpu.SemaphoreType.DMA((16,)),
+            pltpu.SemaphoreType.DMA((18,)),
             pltpu.SemaphoreType.DMA((copies,)),
             pltpu.SemaphoreType.DMA((copies,)),
         ],
@@ -1275,13 +1296,13 @@
 
 def last_kernel(nx, ny, *refs):
     (
-        small_a, small_b, small_c, small_d, middle_ref, tm, sa_ref, sb_ref, keep_hbm, give_hbm, n_hbm,
+        small_a, small_b, small_c, small_d, sa_ref, sb_ref, tm_hbm, middle_hbm, keep_hbm, give_hbm, n_hbm,
         dkv_hbm,
     ) = refs[:12]
     outs = refs[12:22]
     (
         output_ref, kv_ref, first_ref, second_ref, norm_ref, gate_ref, up_ref, down_ref, query_ref, out_ref,
-        nb, dkv, ga, gb, kf, ko, la, lb, fb, lr, kgrid, kgive, kback, sgrid,
+        nb, dkv, tm, middle_ref, kblock, ga, gb, kf, ko, la, lb, fb, lr, kgrid, kgive, kback, sgrid,
         ka0, ka1, kb0, kb1, s0, s1, tka, tkb, ts,
         aa0, aa1, ab0, ab1, kka0, kka1, kkb0, kkb1, ss0, ss1, tt, tk, tsm,
         zsend, zrecv, ksend, krecv, msend, mrecv, y, csend, crecv, kcsend, kcrecv, mcsend, mcrecv,
@@ -1292,8 +1313,8 @@
     halves, k_halves, s_halves = split(r + 3 * rq), split(r // 2), split(r)
     link = Link(ssem, rsem)
     load = fetch(
-        [(give_hbm.at[1], ga), (give_hbm.at[0], gb), (n_hbm, nb), (dkv_hbm, dkv)]
-        + [(keep_hbm.at[1], kf), (keep_hbm.at[0], ko)],
+        [(give_hbm.at[1], ga), (give_hbm.at[0], gb), (keep_hbm.at[1], kf), (n_hbm, nb), (dkv_hbm, dkv)]
+        + [(tm_hbm, tm), (keep_hbm.at[0], ko), (middle_hbm, middle_ref)],
         lsem,
     )
     saved = []
@@ -1321,6 +1342,31 @@
     load[1].wait()
     late_first = link.copy(ga, la, mate)
     late_second = link.copy(gb, lb, mate)
+    for copy in load[2:5]:
+        copy.wait()
+
+    wide = D // nx
+
+    def project(t):
+        kblock[...] = sum(
+            mm(nb[s, :, wide * t : wide * t + wide], dkv[TOK * s : TOK * s + TOK], TN)
+            for s in range(4)
+        ).astype(BF16)
+        for side, target in ((1 - core, kgive), (core, kgrid)):
+            columns = pl.ds(pl.multiple_of(side * QW, QW), QW)
+            block = kblock[:, columns].reshape(ny, 2, r // 2, QW)
+            for h in range(2):
+                target[h, t] = block[:, h]
+
+    project(0)
+    late_first.wait_recv()
+    fb[...] = (kf[...].astype(F32) + la[...].astype(F32)).astype(BF16)
+    late_third = link.copy(fb, lr, far)
+    for t in range(1, nx):
+        project(t)
+    k_copy = link.copy(kgive, kback, mate)
+    for ring in seconds:
+        ring.middle()
     row = iota((8, 1), 0)
     norms = jnp.where(row == 0, small_c[...], jnp.where(row == 1, small_d[...], 0.0))
     small = jnp.concatenate(
@@ -1328,37 +1374,15 @@
     ).T
     sgrid[...] = small.astype(BF16).reshape(nx, ny, r, 128)
     s_ring.start()
-    for copy in load[2:5]:
-        copy.wait()
-    late_first.wait_recv()
-    fb[...] = (kf[...].astype(F32) + la[...].astype(F32)).astype(BF16)
-    late_third = link.copy(fb, lr, far)
-
-    wide = D // nx
-
-    def project(side, target):
-        columns = pl.ds(pl.multiple_of(side * QW, QW), QW)
-        for t in range(nx):
-            block = sum(
-                mm(nb[s, :, wide * t : wide * t + wide], dkv[TOK * s : TOK * s + TOK, columns], TN)
-                for s in range(4)
-            )
-            block = block.astype(BF16).reshape(ny, 2, r // 2, QW)
-            for h in range(2):
-                target[h, t] = block[:, h]
-
-    project(1 - core, kgive)
-    k_copy = link.copy(kgive, kback, mate)
-    for ring in seconds:
-        ring.middle()
-    s_ring.middle()
-    project(core, kgrid)
     k_copy.wait_recv()
     kgrid[...] = (kgrid[...].astype(F32) + kback[...].astype(F32)).astype(BF16)
     for ring in k_rings:
         ring.start()
     for e in range(2):
         seconds[e].end(keeper(tt, halves, e))
+    s_ring.middle()
+    for copy in load[5:]:
+        copy.wait()
 
     fields = [(tm, 0, r), (tm, r, r)] + [(tm, 2 * r + rq * k, rq) for k in range(3)]
     fields += [(tt, 0, r)] + [(tt, r + rq * k, rq) for k in range(3)]
@@ -1419,7 +1443,6 @@
     wsend[:, QW : 2 * QW] = jnp.where(first, k_other, k_own)
     wsend[:, 2 * QW :] = tsm[pl.ds(pl.multiple_of(core * quarter, 8), quarter)] + mcrecv[...]
     w_copy = link.copy(wsend, wrecv, flip("zh"))
-    load[5].wait()
     late_second.wait_recv()
     late_third.wait_recv()
     for j in range(CHUNKS):
@@ -1470,12 +1493,15 @@
     return pl.pallas_call(
         partial(last_kernel, nx, ny),
         out_shape=tuple(jax.ShapeDtypeStruct(*a) for a in results),
-        in_specs=[VSPEC] * 8 + [ANY] * 4,
+        in_specs=[VSPEC] * 6 + [ANY] * 6,
         out_specs=(ANY,) * len(results),
         scratch_shapes=[pltpu.VMEM(*a) for a in results]
         + [
             pltpu.VMEM((4, TOK, D), BF16),
             pltpu.VMEM((4 * TOK, 2 * QW), BF16),
+            pltpu.VMEM((2, mlp_block, 512), F32),
+            pltpu.VMEM((TOK, D), F32),
+            pltpu.VMEM((D // nx, 2 * QW), BF16),
         ]
         + [ROWS_BUF] * 8
         + [
@@ -1514,7 +1540,7 @@
             pltpu.VMEM((r // 4, 128), F32),
             pltpu.VMEM((r // 4, 2 * QW + 128), F32),
             pltpu.VMEM((r // 4, 2 * QW + 128), F32),
-            pltpu.SemaphoreType.DMA((6,)),
+            pltpu.SemaphoreType.DMA((8,)),
             pltpu.SemaphoreType.DMA((len(results),)),
             pltpu.SemaphoreType.DMA((copies,)),
             pltpu.SemaphoreType.DMA((copies,)),
@@ -1563,25 +1589,25 @@
 ):
     nx, ny = lax.axis_size("x"), lax.axis_size("y")
     router_one, router_two = attn_router.T, mlp_router.T
-    normed, keys, values, rows, q, attended, normed_twos, cots, gates, metas, middle = forward_call(
+    normed, keys, values, rows, q, attended, normed_twos, cots, gates, metas, middle, lse = forward_call(
         seg_lengths, seg_parents, slot_order, jnp.swapaxes(attn_routes, 2, 3),
         jnp.swapaxes(mlp_routes, 2, 3), inputs, norm_one, norm_two,
         router_one, cotangent, kv_weight, query_experts, out_experts,
     )
     r, rq = expert_block(nx, ny)
-    grad_middle, grad_norm_two, grad_router_two, sums_a, sums_b, grads_in, keep_out, give_out = mlp_call(
+    grad_norm_two, grad_router_two, sums_a, sums_b, grads_in, keep_out, give_out, grad_middle = mlp_call(
         nx, ny, metas, router_two, norm_two, normed_twos, cotangent, cots, middle,
         gate_experts.reshape(4, nx, ny, r, FF), up_experts.reshape(4, nx, ny, r, FF),
         down_experts.reshape(4, nx, ny, rq, D),
     )
-    grad_norm_one, grad_router_one, grad_kv, sums_mlp, sums_a, sums_b, input_grad = attn_back_call(
-        nx, ny, metas, gates, router_one, norm_one, sums_a, sums_b, inputs, grad_middle, normed,
+    grad_norm_one, grad_router_one, sums_a, sums_b, grad_kv, sums_mlp, input_grad = attn_back_call(
+        nx, ny, metas, gates, lse, router_one, norm_one, sums_a, sums_b, inputs, grad_middle, normed,
         grads_in, keys, values, q, attended, query_experts, out_experts.reshape(4, nx, ny, rq, D),
         kv_weight, rows,
     )
     output, kv, router_one_grad, router_two_grad, norms, gate, up, down, query, out = last_call(
-        nx, ny, grad_router_one, grad_router_two, grad_norm_two, grad_norm_one, middle, sums_mlp, sums_a,
-        sums_b, keep_out, give_out, normed, grad_kv,
+        nx, ny, grad_router_one, grad_router_two, grad_norm_two, grad_norm_one, sums_a, sums_b, sums_mlp,
+        middle, keep_out, give_out, normed, grad_kv,
     )
     (
         output, input_grad, kv, router_one_grad, query, out, router_two_grad, gate, up, down, norm_one_grad,

time: 337 us -> 333 us (0.988)
  Pallas kernels: 327 us -> 323 us
    pallas_call x1, Pallas kernels: 68.5 us -> 63.5 us  [attn_back_call(): pl.pallas_call(partial(attn_back_kernel, nx, ny), out_shape=(jax.ShapeDty...]
where the time goes in v2:
time: 333 us; the launch traced here: 327 us
  Pallas kernels  323 us (97%)
    pallas_call x1, Pallas kernels, forward_call(): pl.pallas_call(forward_kernel, out_shape=(rows, heads, heads, jax.ShapeDt...  131 us
    pallas_call x1, Pallas kernels, mlp_call(): pl.pallas_call(partial(mlp_kernel, nx, ny), out_shape=(jax.ShapeDtypeStru...  74.4 us
    pallas_call x1, Pallas kernels, attn_back_call(): pl.pallas_call(partial(attn_back_kernel, nx, ny), out_shape=(jax.ShapeDty...  63.5 us
    pallas_call x1, Pallas kernels, last_call(): pl.pallas_call(partial(last_kernel, nx, ny), out_shape=tuple((jax.ShapeDt...  49.9 us

profile of v2, /device:TPU:1, one launch (start us, length us, event | category | flops | bytes accessed | tf_op | source)
XLA Modules:
  0.0 326.9 jit_solution(3759761839838610933)
XLA Ops:
  0.6 130.9 %attention_forward.1 = (bf16[4,384,1536]{2,1,0:T(8,128)(2,1)}, bf16[4,384,512]{2,1,0:T(8,128)(2,1)}, bf16[4,384,512]{2,1,0:T(8,128)(2,1)}, bf16[2,512,1536]{2,1,...) custom-call(s32[1,2,13]{2,1,0:T(2,128)} %refs_0_.1, ...), custom_call_target="tpu_custom_call" | custom-call | flops 1000000000 | bytes 300000000 | tf_op jit(solution)/shard_map/attention_forward/pallas_call | solution.py:642
  131.6 74.4 %feed_forward.1 = (f32[1,1536]{1,0:T(1,128)}, f32[8,1536]{1,0:T(8,128)}, bf16[2,4,144,512]{3,2,1,0:T(8,128)(2,1)}, bf16[2,4,144,512]{3,2,1,0:T(8,128)(2,1)}, bf1...) custom-call(s32[4,8,384]{2,1,0:T(8,128)} %get-tuple-element.61.refs_, ...), custom_call_target="tpu_custom_call" | custom-call | flops 1000000000 | bytes 250000000 | tf_op jit(solution)/shard_map/feed_forward/pallas_call | solution.py:899
  206.0 63.5 %attention_backward.1 = (f32[1,1536]{1,0:T(1,128)}, f32[8,1536]{1,0:T(8,128)}, bf16[4,192,512]{2,1,0:T(8,128)(2,1)}, bf16[4,192,512]{2,1,0:T(8,128)(2,1)}, bf16[...) custom-call(s32[4,8,384]{2,1,0:T(8,128)} %get-tuple-element.61.refs_0_, ...), custom_call_target="tpu_custom_call" | custom-call | flops 1000000000 | bytes 300000000 | tf_op jit(solution)/shard_map/attention_backward/pallas_call | solution.py:1238
  269.5 49.9 %last_sums.1 = (bf16[384,1536]{1,0:T(8,128)(2,1)}, f32[12,1024]{1,0:T(8,128)}, f32[12,8]{1,0:T(8,128)}, f32[12,8]{1,0:T(8,128)}, f32[8,12]{1,0:T(8,128)}, /*inde...) custom-call(f32[8,1536]{1,0:T(8,128)} %get-tuple-element.77.refs_0_,, ...), custom_call_target="tpu_custom_call" | custom-call | flops 1000000000 | bytes 150000000 | tf_op jit(solution)/shard_map/last_sums/pallas_call | solution.py:1493
  319.4 4.4 %results.1 = (bf16[384,1536]{1,0:T(8,128)(2,1)}, bf16[384,1536]{1,0:T(8,128)(2,1)}, f32[12,1024]{1,0:T(8,128)}, f32[12,8]{1,0:T(8,128)}, f32[4,24,512]{2,1,0:T(8...) custom-call(f32[8,12]{1,0:T(8,128)} %get-tuple-element.87.norms_ref,, ...), custom_call_target="tpu_custom_call" | custom-call | tf_op jit(solution)/shard_map/results/pallas_call | solution.py:1572
  323.8 1.4 copy.29
  325.1 1.4 copy.30

commit v3 on v2

--- a/solution.py
+++ b/solution.py
@@ -1134,10 +1134,11 @@
             if s == 1:
                 collect.send_mate()
 
-    for copy in load[:5]:
-        copy.wait()
+    load[0].wait()
     spread(3)
     spread(2)
+    for copy in load[1:5]:
+        copy.wait()
     outward(2)
     for copy in load[5:10]:
         copy.wait()
@@ -1173,11 +1174,11 @@
     saved = []
 
     def save(source, target):
-        copy = pltpu.make_async_copy(source, target, lsem.at[15 + len(saved)])
+        copy = pltpu.make_async_copy(source, target, lsem.at[17 + len(saved)])
         copy.start()
         saved.append(copy)
 
-    rows_load = pltpu.make_async_copy(r_hbm, dr, lsem.at[14])
+    rows_load = pltpu.make_async_copy(r_hbm, dr, lsem.at[16])
     rows_load.start()
     pairs.forward()
     scores_back(1)
@@ -1200,7 +1201,7 @@
     for ring, out in zip(o_rings, (oa_ref, ob_ref)):
         ring.end(keeper(out, o_halves))
 
-    for copy in load[11:]:
+    for copy in load[11:14]:
         copy.wait()
     logits = logit_grads(mbuf[0], 0, gbuf[0], pairs.total())
     router_grad_ref[...] = mm(logits, normed[...])
@@ -1284,7 +1285,7 @@
         + (ring_buffers((ny,), block) + ring_buffers((nx,), block)) * 2
         + ring_buffers((), mlp_block // 2) * 4
         + [
-            pltpu.SemaphoreType.DMA((18,)),
+            pltpu.SemaphoreType.DMA((20,)),
             pltpu.SemaphoreType.DMA((copies,)),
             pltpu.SemaphoreType.DMA((copies,)),
         ],
@@ -1305,8 +1306,7 @@
         nb, dkv, tm, middle_ref, kblock, ga, gb, kf, ko, la, lb, fb, lr, kgrid, kgive, kback, sgrid,
         ka0, ka1, kb0, kb1, s0, s1, tka, tkb, ts,
         aa0, aa1, ab0, ab1, kka0, kka1, kkb0, kkb1, ss0, ss1, tt, tk, tsm,
-        zsend, zrecv, ksend, krecv, msend, mrecv, y, csend, crecv, kcsend, kcrecv, mcsend, mcrecv,
-        wsend, wrecv, lsem, osem, ssem, rsem,
+        zsend, zrecv, y, csend, crecv, pieces, landed, lsem, osem, ssem, rsem,
     ) = refs[22:]
     zl, core, zh = lax.axis_index("zl"), lax.axis_index("c"), lax.axis_index("zh")
     r, rq = expert_block(nx, ny)
@@ -1326,7 +1326,8 @@
             saved.append(copy)
 
     mate, far = flip("c"), flip("zl", "zh")
-    greet([mate, far, flip("zl"), flip("zh")] + around(("x", "y")))
+    column = ["c"], ["zl"], ["zh"], ["c", "zl"], ["c", "zh"], ["zl", "zh"], ["c", "zl", "zh"]
+    greet([flip(*axes) for axes in column] + around(("x", "y")))
     seconds = [
         Ring(link, "y", lambda i, h: sa_ref.at[i, halves[h]], aa0, aa1),
         Ring(link, "x", lambda i, h: sb_ref.at[i, halves[h]], ab0, ab1),
@@ -1358,6 +1359,7 @@
             for h in range(2):
                 target[h, t] = block[:, h]
 
+    pieces[...] = jnp.zeros_like(pieces)
     project(0)
     late_first.wait_recv()
     fb[...] = (kf[...].astype(F32) + la[...].astype(F32)).astype(BF16)
@@ -1420,29 +1422,28 @@
     s_second.end(store_small)
     for e in range(2):
         k_seconds[e].end(keeper(tk, k_halves, e))
-    ksend[...] = tk[1 - zl].astype(BF16)
-    msend[...] = tsm[pl.ds(pl.multiple_of((1 - zl) * (r // 2), 8), r // 2)].astype(BF16)
-    k_copies = [link.copy(a, b, to_zl) for a, b in ((ksend, krecv), (msend, mrecv))]
-    for copy in k_copies:
-        copy.wait_recv()
-    k_own = tk[zl] + krecv[...].astype(F32)
-    m_own = tsm[pl.ds(pl.multiple_of(zl * (r // 2), 8), r // 2)] + mrecv[...].astype(F32)
-    tk[0] = k_own
-    tsm[0 : r // 2] = m_own
-
-    quarter = r // 4
-    kcsend[...] = tk[0, pl.ds(pl.multiple_of((1 - core) * quarter, 8), quarter)]
-    mcsend[...] = tsm[pl.ds(pl.multiple_of((1 - core) * quarter, 8), quarter)]
-    m_copies = [link.copy(a, b, mate) for a, b in ((kcsend, kcrecv), (mcsend, mcrecv))]
-    for copy in m_copies:
-        copy.wait_recv()
-    k_own = tk[0, pl.ds(pl.multiple_of(core * quarter, 8), quarter)]
-    k_other = kcrecv[...]
-    first = core == 0
-    wsend[:, 0:QW] = jnp.where(first, k_own, k_other)
-    wsend[:, QW : 2 * QW] = jnp.where(first, k_other, k_own)
-    wsend[:, 2 * QW :] = tsm[pl.ds(pl.multiple_of(core * quarter, 8), quarter)] + mcrecv[...]
-    w_copy = link.copy(wsend, wrecv, flip("zh"))
+
+    piece = r // 8
+    for p in range(8):
+        rows = slice(piece * (p % 4), piece * (p % 4) + piece)
+        pieces[p, 0:piece, 0:QW] = tk[p // 4, rows]
+        pieces[p, 0:piece, QW:] = tsm[piece * p : piece * p + piece]
+
+    def other(m):
+        return (
+            lax.rem(zl + m // 4, 2), lax.rem(core + m // 2 % 2, 2), lax.rem(zh + m % 2, 2)
+        )
+
+    p_copies = []
+    for m in range(1, 8):
+        at = other(m)
+        p_copies.append(
+            link.copy(
+                pieces.at[4 * at[0] + 2 * at[1] + at[2]],
+                landed.at[m],
+                {"zl": at[0], "c": at[1], "zh": at[2]},
+            )
+        )
     late_second.wait_recv()
     late_third.wait_recv()
     for j in range(CHUNKS):
@@ -1453,17 +1454,23 @@
             + lr[part(j)].astype(F32)
         ).astype(BF16)
     save(0)
-    w_copy.wait_recv()
-    total = wsend[...] + wrecv[...]
-    total = jnp.where(zh == 0, total[0 : r // 8], total[r // 8 :])
-    kv_ref[...] = total[:, 0 : 2 * QW]
-    first_ref[...] = total[:, 2 * QW : 2 * QW + 8]
-    second_ref[...] = total[:, 2 * QW + 8 : 2 * QW + 16]
-    norm_ref[...] = total[:, 2 * QW : 2 * QW + 128].T[16:24]
+    for copy in p_copies:
+        copy.wait_recv()
+    mine = pieces[4 * zl + 2 * core + zh]
+    own_half = mine + landed[1] + landed[4] + landed[5]
+    other_half = landed[2] + landed[3] + landed[6] + landed[7]
+    first = core == 0
+    kv_ref[:, 0:QW] = jnp.where(first, own_half, other_half)[0:piece, 0:QW]
+    kv_ref[:, QW:] = jnp.where(first, other_half, own_half)[0:piece, 0:QW]
+    total = (own_half + other_half)[:, QW:]
+    total = total.T
+    first_ref[...] = total[0:8, 0:piece]
+    second_ref[...] = total[8:16, 0:piece]
+    norm_ref[...] = total[16:24, 0:piece]
     save(1, 2, 3, 4)
     for ring in seconds + k_rings + [s_ring] + k_seconds + [s_second]:
         ring.close()
-    for copy in [late_first, late_second, late_third, k_copy, z_copy, c_copy, w_copy] + k_copies + m_copies:
+    for copy in [late_first, late_second, late_third, k_copy, z_copy, c_copy] + p_copies:
         copy.wait_send()
     for copy in saved:
         copy.wait()
@@ -1477,12 +1484,12 @@
     def small_buffers(lead):
         return [pltpu.VMEM((3,) + lead + (s.stop - s.start, 128), BF16) for s in split(r)]
 
-    copies = 4 * 12 + 11
+    copies = 4 * 12 + 13
     results = [
         ((TOK, D), BF16),
         ((r // 8, 2 * QW), F32),
-        ((r // 8, 8), F32),
-        ((r // 8, 8), F32),
+        ((8, r // 8), F32),
+        ((8, r // 8), F32),
         ((8, r // 8), F32),
         ((4, r // 4, FF), F32),
         ((4, r // 4, FF), F32),
@@ -1527,19 +1534,11 @@
             pltpu.VMEM((r, 128), F32),
             pltpu.VMEM((2, zrows, 512), BF16),
             pltpu.VMEM((2, zrows, 512), BF16),
-            pltpu.VMEM((k_block, 512), BF16),
-            pltpu.VMEM((k_block, 512), BF16),
-            pltpu.VMEM((r // 2, 128), BF16),
-            pltpu.VMEM((r // 2, 128), BF16),
             pltpu.VMEM((2, zrows, 512), F32),
             pltpu.VMEM((2, zrows // 2, 512), F32),
             pltpu.VMEM((2, zrows // 2, 512), F32),
-            pltpu.VMEM((r // 4, 512), F32),
-            pltpu.VMEM((r // 4, 512), F32),
-            pltpu.VMEM((r // 4, 128), F32),
-            pltpu.VMEM((r // 4, 128), F32),
-            pltpu.VMEM((r // 4, 2 * QW + 128), F32),
-            pltpu.VMEM((r // 4, 2 * QW + 128), F32),
+            pltpu.VMEM((8, (r // 8 + 7) // 8 * 8, QW + 128), F32),
+            pltpu.VMEM((8, (r // 8 + 7) // 8 * 8, QW + 128), F32),
             pltpu.SemaphoreType.DMA((8,)),
             pltpu.SemaphoreType.DMA((len(results),)),
             pltpu.SemaphoreType.DMA((copies,)),
@@ -1552,17 +1551,23 @@
 
 
 def copy_kernel(norms_ref, *refs):
-    n = (len(refs) - 4) // 3
-    sources, targets, (first, second), bufs = refs[:n], refs[n : 2 * n], refs[2 * n : 2 * n + 2], refs[2 * n + 2 : -2]
+    n = (len(refs) - 6) // 3
+    sources, targets, vectors = refs[:n], refs[n : 2 * n], refs[2 * n : 2 * n + 2]
+    bufs, held = refs[2 * n + 2 : 3 * n + 2], refs[3 * n + 2 : 3 * n + 4]
     came = fetch(list(zip(sources, bufs)), refs[-2])
-    first[...] = norms_ref[1]
-    second[...] = norms_ref[0]
     left = []
+
+    def leave(source, target):
+        copy = pltpu.make_async_copy(source, target, refs[-1].at[len(left)])
+        copy.start()
+        left.append(copy)
+
+    for k in range(2):
+        held[k][...] = norms_ref[1 - k]
+        leave(held[k], vectors[k])
     for k in range(n):
         came[k].wait()
-        copy = pltpu.make_async_copy(bufs[k], targets[k], refs[-1].at[k])
-        copy.start()
-        left.append(copy)
+        leave(bufs[k], targets[k])
     for copy in left:
         copy.wait()
 
@@ -1574,9 +1579,10 @@
         out_shape=tuple(jax.ShapeDtypeStruct(a.shape, a.dtype) for a in arrays)
         + (jax.ShapeDtypeStruct((count,), F32),) * 2,
         in_specs=[VSPEC] + [ANY] * n,
-        out_specs=(ANY,) * n + (VSPEC,) * 2,
+        out_specs=(ANY,) * (n + 2),
         scratch_shapes=[pltpu.VMEM(a.shape, a.dtype) for a in arrays]
-        + [pltpu.SemaphoreType.DMA((n,)), pltpu.SemaphoreType.DMA((n,))],
+        + [pltpu.VMEM((count,), F32)] * 2
+        + [pltpu.SemaphoreType.DMA((n,)), pltpu.SemaphoreType.DMA((n + 2,))],
         compiler_params=params(60),
         name="results",
     )(norms, *arrays)
@@ -1616,8 +1622,8 @@
         norms, output, input_grad, kv, router_one_grad, query, out, router_two_grad, gate, up, down
     )
     return (
-        output, input_grad, norm_one_grad, kv, router_one_grad, query, out, norm_two_grad,
-        router_two_grad, gate, up, down,
+        output, input_grad, norm_one_grad, kv, router_one_grad.T, query, out, norm_two_grad,
+        router_two_grad.T, gate, up, down,
     )
 
 

time: 333 us -> 326 us (0.979)
  Pallas kernels: 323 us -> 319 us
    pallas_call x1, Pallas kernels: 49.9 us -> 46.2 us  [last_call(): pl.pallas_call(partial(last_kernel, nx, ny), out_shape=tuple((jax.ShapeDt...]
where the time goes in v3:
time: 326 us; the launch traced here: 320 us
  Pallas kernels  319 us (98%)
    pallas_call x1, Pallas kernels, forward_call(): pl.pallas_call(forward_kernel, out_shape=(rows, heads, heads, jax.ShapeDt...  131 us
    pallas_call x1, Pallas kernels, mlp_call(): pl.pallas_call(partial(mlp_kernel, nx, ny), out_shape=(jax.ShapeDtypeStru...  74.4 us
    pallas_call x1, Pallas kernels, attn_back_call(): pl.pallas_call(partial(attn_back_kernel, nx, ny), out_shape=(jax.ShapeDty...  63.5 us
    pallas_call x1, Pallas kernels, last_call(): pl.pallas_call(partial(last_kernel, nx, ny), out_shape=tuple((jax.ShapeDt...  46.2 us

profile of v3, /device:TPU:1, one launch (start us, length us, event | category | flops | bytes accessed | tf_op | source)
XLA Modules:
  0.0 320.0 jit_solution(6532721776306360518)
XLA Ops:
  0.6 130.9 %attention_forward.1 = (bf16[4,384,1536]{2,1,0:T(8,128)(2,1)}, bf16[4,384,512]{2,1,0:T(8,128)(2,1)}, bf16[4,384,512]{2,1,0:T(8,128)(2,1)}, bf16[2,512,1536]{2,1,...) custom-call(s32[1,2,13]{2,1,0:T(2,128)} %refs_0_.1, ...), custom_call_target="tpu_custom_call" | custom-call | flops 1000000000 | bytes 300000000 | tf_op jit(solution)/shard_map/attention_forward/pallas_call | solution.py:642
  131.6 74.4 %feed_forward.1 = (f32[1,1536]{1,0:T(1,128)}, f32[8,1536]{1,0:T(8,128)}, bf16[2,4,144,512]{3,2,1,0:T(8,128)(2,1)}, bf16[2,4,144,512]{3,2,1,0:T(8,128)(2,1)}, bf1...) custom-call(s32[4,8,384]{2,1,0:T(8,128)} %get-tuple-element.61.refs_, ...), custom_call_target="tpu_custom_call" | custom-call | flops 1000000000 | bytes 250000000 | tf_op jit(solution)/shard_map/feed_forward/pallas_call | solution.py:899
  206.0 63.5 %attention_backward.1 = (f32[1,1536]{1,0:T(1,128)}, f32[8,1536]{1,0:T(8,128)}, bf16[4,192,512]{2,1,0:T(8,128)(2,1)}, bf16[4,192,512]{2,1,0:T(8,128)(2,1)}, bf16[...) custom-call(s32[4,8,384]{2,1,0:T(8,128)} %get-tuple-element.61.refs_0_, ...), custom_call_target="tpu_custom_call" | custom-call | flops 1000000000 | bytes 300000000 | tf_op jit(solution)/shard_map/attention_backward/pallas_call | solution.py:1239
  269.5 46.2 %last_sums.1 = (bf16[384,1536]{1,0:T(8,128)(2,1)}, f32[12,1024]{1,0:T(8,128)}, f32[8,12]{1,0:T(8,128)}, f32[8,12]{1,0:T(8,128)}, f32[8,12]{1,0:T(8,128)}, /*inde...) custom-call(f32[8,1536]{1,0:T(8,128)} %get-tuple-element.77.refs_0_,, ...), custom_call_target="tpu_custom_call" | custom-call | flops 1000000000 | bytes 150000000 | tf_op jit(solution)/shard_map/last_sums/pallas_call | solution.py:1500
  315.7 3.9 %results.1 = (bf16[384,1536]{1,0:T(8,128)(2,1)}, bf16[384,1536]{1,0:T(8,128)(2,1)}, f32[12,1024]{1,0:T(8,128)}, f32[8,12]{1,0:T(8,128)}, f32[4,24,512]{2,1,0:T(8...) custom-call(f32[8,12]{1,0:T(8,128)} %get-tuple-element.87.norms_ref,, ...), custom_call_target="tpu_custom_call" | custom-call | tf_op jit(solution)/shard_map/results/pallas_call | solution.py:1577
